TPU v7x, 512 devices: a whole 4x8x8 slice. The times are simulated.
512 devices in a mesh: tm: 64 (over z, y), state: 8 (over x, core).
Axes of the slice: x: 4, y: 8, z: 8, core: 2. Of those that a mesh axis runs over, the one named last changes fastest.
Arguments:
- diagonal: float32 [128, 256, 256], P('tm', 'state'), may hold values from -1 to 12, as said below
- coupling: float32 [128, 256, 256], P('tm', 'state'), may hold values from -1.6 to 0.6, as said below
- info: float32 [128, 256], P('tm', 'state'), may hold values from -19 to 19
Outputs:
- smoothed: float32 [128, 256], P('tm', 'state')
Inputs may be any that keep to these rules, and one draw needn't show every extreme that they name: Each diagonal block is symmetric, and the matrix J built from diagonal and coupling is positive definite. `coupling`: together with diagonal it forms a positive definite J.
All inputs are finite; a program needn't handle non-finite values.
Results may differ from a plain program's by a relative error of at most 0.0022.
Values sent between devices are 32-bit elements; how exact they have to be, the bound alone decides.
A program may use at most 64 MiB of HBM per device.

v0:
```python
import jax
import jax.numpy as jnp
from jax import lax
from jax.sharding import PartitionSpec as P


def from_behind(shard, axis, by):
    peers = lax.axis_size(axis)
    pairs = [(i, i + by) for i in range(peers) if 0 <= i + by < peers]
    return lax.ppermute(shard, axis, pairs)


def solve_with(factor, right_side):
    return jax.scipy.linalg.cho_solve((factor, True), right_side)


def body(diagonal, coupling, info):
    exact = lax.Precision.HIGHEST
    seg_steps = diagonal.shape[0]
    panel_rows = diagonal.shape[1]
    width = diagonal.shape[2]
    tm_index = lax.axis_index("tm")
    tm_count = lax.axis_size("tm")
    offset = lax.axis_index("state") * panel_rows
    edge_rows = jnp.where(
        tm_index == tm_count - 1, jnp.zeros_like(coupling[seg_steps - 1]), coupling[seg_steps - 1]
    )
    whole_a, whole_r, whole_h = (
        lax.all_gather(diagonal[seg_steps - 1], "state", axis=0, tiled=True),
        lax.all_gather(edge_rows, "state", axis=0, tiled=True),
        lax.all_gather(info[seg_steps - 1], "state", axis=0, tiled=True),
    )
    sum_a = jnp.zeros((width, width), jnp.float32)
    sum_h = jnp.zeros((width,), jnp.float32)
    prior_a = lax.all_gather(diagonal[0], "state", axis=0, tiled=True)
    link_block = lax.all_gather(coupling[0], "state", axis=0, tiled=True)
    prior_h = lax.all_gather(info[0], "state", axis=0, tiled=True)
    factor = jnp.linalg.cholesky(whole_a)
    solved = solve_with(factor, jnp.concatenate([link_block.T, whole_r], axis=1))
    toward_lower = solved[:, :width]
    toward_upper = solved[:, width:]
    mean_part = solve_with(factor, whole_h)
    kept_blocks = [(factor, link_block, whole_r, whole_h)]
    sum_a = sum_a - jnp.dot(whole_r.T, toward_upper, precision=exact)
    sum_h = sum_h - jnp.dot(whole_r.T, mean_part, precision=exact)
    whole_a = prior_a - jnp.dot(link_block, toward_lower, precision=exact)
    whole_r = -jnp.dot(link_block, toward_upper, precision=exact)
    whole_h = prior_h - jnp.dot(link_block, mean_part, precision=exact)
    own_a = lax.dynamic_slice_in_dim(whole_a, offset, panel_rows, 0)
    own_c = lax.dynamic_slice_in_dim(whole_r, offset, panel_rows, 0)
    own_h = lax.dynamic_slice_in_dim(whole_h, offset, panel_rows, 0)
    right_a = lax.dynamic_slice_in_dim(sum_a, offset, panel_rows, 0)
    right_h = lax.dynamic_slice_in_dim(sum_h, offset, panel_rows, 0)
    carried_a, carried_h = from_behind((right_a, right_h), "tm", 1)
    block_a = own_a + carried_a
    block_c = own_c
    block_h = own_h + carried_h
    saved_factor = jnp.eye(width, dtype=jnp.float32)
    saved_lower = jnp.zeros((width, width), jnp.float32)
    saved_upper = jnp.zeros((width, width), jnp.float32)
    saved_info = jnp.zeros((width,), jnp.float32)
    distances = [2**level for level in range(tm_count.bit_length() - 1)]
    for distance in distances:
        is_odd = tm_index % (2 * distance) == distance
        is_kept = tm_index % (2 * distance) == 0
        weight = is_odd.astype(jnp.float32)
        full_a, full_c, full_h = (
            lax.all_gather(block_a, "state", axis=0, tiled=True),
            lax.all_gather(block_c, "state", axis=0, tiled=True),
            lax.all_gather(block_h, "state", axis=0, tiled=True),
        )
        factor = jnp.linalg.cholesky(full_a)
        upper_part = solve_with(factor, lax.dynamic_slice_in_dim(full_c, offset, panel_rows, 1))
        upward_a = -weight * jnp.dot(upper_part.T, full_c, precision=exact)
        upward_h = -weight * jnp.dot(upper_part.T, full_h, precision=exact)
        dense_precision, got_a, got_h = from_behind((full_c, upward_a, upward_h), "tm", distance)
        lower_rows = lax.dynamic_slice_in_dim(dense_precision, offset, panel_rows, 0)
        lower_part = solve_with(factor, lower_rows.T)
        left_a = -jnp.dot(lower_part.T, dense_precision.T, precision=exact)
        left_c = -jnp.dot(lower_part.T, full_c, precision=exact)
        left_h = -jnp.dot(lower_part.T, full_h, precision=exact)
        from_above = from_behind(
            (weight * left_a, weight * left_c, weight * left_h), "tm", -distance
        )
        saved_factor = jnp.where(is_odd, factor, saved_factor)
        saved_lower = jnp.where(is_odd, dense_precision, saved_lower)
        saved_upper = jnp.where(is_odd, full_c, saved_upper)
        saved_info = jnp.where(is_odd, full_h, saved_info)
        block_a = jnp.where(is_kept, block_a + from_above[0] + got_a, block_a)
        block_c = jnp.where(is_kept, from_above[1], block_c)
        block_h = jnp.where(is_kept, block_h + from_above[2] + got_h, block_h)
    root_a, root_h = (
        lax.all_gather(block_a, "state", axis=0, tiled=True),
        lax.all_gather(block_h, "state", axis=0, tiled=True),
    )
    root_x = solve_with(jnp.linalg.cholesky(root_a), root_h)
    estimate = jnp.where(tm_index == 0, root_x, jnp.zeros_like(root_x))
    upper_x = jnp.zeros_like(root_x)
    for distance in reversed(distances):
        is_odd = tm_index % (2 * distance) == distance
        below, above = from_behind((estimate, upper_x), "tm", distance)
        residual = (
            saved_info
            - jnp.dot(saved_lower.T, below, precision=exact)
            - jnp.dot(saved_upper, above, precision=exact)
        )
        estimate = jnp.where(is_odd, solve_with(saved_factor, residual), estimate)
        upper_x = from_behind(estimate, "tm", -distance)
    states = [estimate]
    previous = estimate
    for factor, link_block, onward, vector in reversed(kept_blocks):
        residual = (
            vector
            - jnp.dot(link_block.T, previous, precision=exact)
            - jnp.dot(onward, upper_x, precision=exact)
        )
        previous = solve_with(factor, residual)
        states.append(previous)
    return jnp.stack(
        [lax.dynamic_slice_in_dim(value, offset, panel_rows, 0) for value in states], axis=0
    )


def solution(mesh):
    placed = (P("tm", "state", None), P("tm", "state", None), P("tm", "state"))
    return jax.shard_map(
        body, mesh=mesh, in_specs=placed, out_specs=P("tm", "state"), check_vma=False
    )
```

profile of v0, /device:TPU:248, one launch (start us, length us, event | category | flops | bytes accessed | tf_op | source)
XLA Modules:
  0.0 1160.4 jit_solution(10615939912034535617)
XLA Ops:
  13.9 13.2 %all-gather.3 = f32[1,256,256]{2,0,1:T(1,128)S(1)} all-gather(f32[1,32,256]{2,0,1:T(1,128)S(1)} %broadcast_select_fusion), channel_id=5, replica_groups=mesh['tm'=64,'state'=8] {'state'}, dimensions={1}, use_global_device_ids=true | all-gather | bytes 294912 | tf_op jit(solution)/shard_map/all_gather | solution.py:30
  27.1 12.8 %all-gather.1 = f32[1,256,256]{2,0,1:T(1,128)S(1)} all-gather(f32[1,32,256]{2,0,1:T(1,128)S(1)} %copy.114), channel_id=3, replica_groups=mesh['tm'=64,'state'=8] {'state'}, dimensions={1}, use_global_device_ids=true | all-gather | bytes 294912 | tf_op jit(solution)/shard_map/all_gather | solution.py:29
  40.1 11.7 %cholesky.382 = f32[128,128]{1,0:T(8,128)S(1)} custom-call(f32[128,128]{1,0:T(8,128)S(1)} %cholesky.650), custom_call_target="Cholesky" | custom-call | tf_op jit(solution)/shard_map/jit(cholesky)/cholesky | solution.py:38
  62.2 11.7 %cholesky.399 = f32[128,128]{1,0:T(8,128)S(1)} custom-call(f32[128,128]{1,0:T(8,128)S(1)} %convolution_subtract_fusion.8), custom_call_target="Cholesky" | custom-call | tf_op jit(solution)/shard_map/jit(cholesky)/cholesky | solution.py:38
  80.1 19.7 %custom-call.25 = f32[2,128,128]{1,2,0:T(8,128)S(1)} custom-call(f32[2,128,128]{2,1,0:T(8,128)S(1)} %get-tuple-element.31), custom_call_target="InvertDiagBlocksLowerTriangular" | custom-call | tf_op jit(solution)/shard_map/jit(_cho_solve)/triangular_solve | solution.py:14
  99.7 14.8 %all-reduce.10 = (f32[256]{0:T(256)S(1)}, f32[256]{0:T(256)S(1)}) all-reduce(f32[256]{0:T(256)S(1)} %bitcast_dynamic-update-slice_fusion.9, f32[256]{0:T(256)S(1)} %bitcast_dynamic-update-slice_fusion.10), channel_id=7, replica_groups=mesh['tm'=64,'state'=8] {'state'}, use_global_device_ids=true, to_apply=%add.2 | all-reduce | flops 512 | bytes 4096 | tf_op jit(solution)/shard_map/all_gather | solution.py:31
  118.4 12.8 %all-gather.2 = f32[1,256,256]{2,0,1:T(1,128)S(1)} all-gather(f32[1,32,256]{2,0,1:T(1,128)S(1)} %copy.115), channel_id=4, replica_groups=mesh['tm'=64,'state'=8] {'state'}, dimensions={1}, use_global_device_ids=true | all-gather | bytes 294912 | tf_op jit(solution)/shard_map/all_gather | solution.py:36
  137.0 12.8 %all_gather.83 = f32[256,256]{1,0:T(8,128)S(1)} all-gather(f32[32,256]{1,0:T(8,128)S(1)} %fusion.247), channel_id=1, replica_groups=mesh['tm'=64,'state'=8] {'state'}, dimensions={0}, use_global_device_ids=true | all-gather | bytes 294912 | tf_op jit(solution)/shard_map/all_gather | solution.py:69
  152.7 12.8 %all-gather = f32[1,256,256]{2,0,1:T(1,128)S(1)} all-gather(f32[1,32,256]{2,0,1:T(1,128)S(1)} %copy.113), channel_id=2, replica_groups=mesh['tm'=64,'state'=8] {'state'}, dimensions={1}, use_global_device_ids=true | all-gather | bytes 294912 | tf_op jit(solution)/shard_map/all_gather | solution.py:35
  165.9 12.7 %all-reduce.3 = f32[256]{0:T(256)S(1)} all-reduce(f32[256]{0:T(256)S(1)} %fusion.383), channel_id=1, replica_groups=mesh['tm'=64,'state'=8] {'state'}, use_global_device_ids=true, to_apply=%add.3 | all-reduce | flops 256 | bytes 2048
  178.7 13.2 %all_gather.82 = f32[256,256]{1,0:T(8,128)S(1)} all-gather(f32[32,256]{1,0:T(8,128)S(1)} %fusion.248), channel_id=1, replica_groups=mesh['tm'=64,'state'=8] {'state'}, dimensions={0}, use_global_device_ids=true | all-gather | bytes 294912 | tf_op jit(solution)/shard_map/all_gather | solution.py:68
  192.2 11.7 %cholesky.416 = f32[128,128]{1,0:T(8,128)S(1)} custom-call(f32[128,128]{1,0:T(8,128)S(1)} %cholesky.654), custom_call_target="Cholesky" | custom-call | tf_op jit(solution)/shard_map/jit(cholesky)/cholesky | solution.py:72
  214.9 11.7 %cholesky.433 = f32[128,128]{1,0:T(8,128)S(1)} custom-call(f32[128,128]{1,0:T(8,128)S(1)} %slice_subtract_fusion), custom_call_target="Cholesky" | custom-call | tf_op jit(solution)/shard_map/jit(cholesky)/cholesky | solution.py:72
  232.7 19.7 %custom-call.54 = f32[2,128,128]{1,2,0:T(8,128)S(1)} custom-call(f32[2,128,128]{2,1,0:T(8,128)S(1)} %get-tuple-element.146), custom_call_target="InvertDiagBlocksLowerTriangular" | custom-call | tf_op jit(solution)/shard_map/jit(_cho_solve)/triangular_solve | solution.py:14
  262.5 14.5 %collective-permute-start.21 = (f32[32]{0:T(128)S(1)}, f32[32]{0:T(128)S(1)}, u32[]{:S(2)}, u32[]{:S(2)}) collective-permute-start(f32[32]{0:T(128)S(1)} %fusion.42), channel_id=1, source_target_pairs={{8,0},{16,8},{24,16},{32,24},{40,32},{48,40},{56,48},{64,56},{72,6... | collective-permute-start | bytes 392 | tf_op jit(solution)/shard_map/ppermute | solution.py:10
  280.7 15.9 %collective-permute-start.4 = (f32[32,256]{1,0:T(8,128)S(1)}, f32[32,256]{1,0:T(8,128)S(1)}, u32[]{:S(2)}, u32[]{:S(2)}) collective-permute-start(f32[32,256]{1,0:T(8,128)S(1)} %fusion.9), channel_id=1, source_target_pairs={{8,0},{16,8},{24,16},{32,24},{40,32},{48,40},{56,48},{64,56},{72,6... | collective-permute-start | bytes 98312 | tf_op jit(solution)/shard_map/ppermute | solution.py:10
  296.8 14.9 %all-reduce.4 = f32[256]{0:T(256)S(1)} all-reduce(f32[256]{0:T(256)S(1)} %get-tuple-element.335), channel_id=1, replica_groups=mesh['tm'=64,'state'=8] {'state'}, use_global_device_ids=true, to_apply=%add.4 | all-reduce | flops 256 | bytes 2048
  311.7 12.8 %all_gather.85 = f32[256,256]{1,0:T(8,128)S(1)} all-gather(f32[32,256]{1,0:T(8,128)S(1)} %broadcast_select_fusion.1), channel_id=1, replica_groups=mesh['tm'=64,'state'=8] {'state'}, dimensions={0}, use_global_device_ids=true | all-gather | bytes 294912 | tf_op jit(solution)/shard_map/all_gather | solution.py:69
  330.3 12.8 %all_gather.84 = f32[256,256]{1,0:T(8,128)S(1)} all-gather(f32[32,256]{1,0:T(8,128)S(1)} %add_select_fusion.5), channel_id=1, replica_groups=mesh['tm'=64,'state'=8] {'state'}, dimensions={0}, use_global_device_ids=true | all-gather | bytes 294912 | tf_op jit(solution)/shard_map/all_gather | solution.py:68
  343.3 11.7 %cholesky.450 = f32[128,128]{1,0:T(8,128)S(1)} custom-call(f32[128,128]{1,0:T(8,128)S(1)} %cholesky.657), custom_call_target="Cholesky" | custom-call | tf_op jit(solution)/shard_map/jit(cholesky)/cholesky | solution.py:72
  366.1 11.7 %cholesky.467 = f32[128,128]{1,0:T(8,128)S(1)} custom-call(f32[128,128]{1,0:T(8,128)S(1)} %convolution_subtract_fusion.7), custom_call_target="Cholesky" | custom-call | tf_op jit(solution)/shard_map/jit(cholesky)/cholesky | solution.py:72
  384.2 19.7 %custom-call.57 = f32[2,128,128]{1,2,0:T(8,128)S(1)} custom-call(f32[2,128,128]{2,1,0:T(8,128)S(1)} %get-tuple-element.148), custom_call_target="InvertDiagBlocksLowerTriangular" | custom-call | tf_op jit(solution)/shard_map/jit(_cho_solve)/triangular_solve | solution.py:14
  426.2 12.7 %all-reduce.5 = f32[256]{0:T(256)S(1)} all-reduce(f32[256]{0:T(256)S(1)} %get-tuple-element.333), channel_id=1, replica_groups=mesh['tm'=64,'state'=8] {'state'}, use_global_device_ids=true, to_apply=%add.5 | all-reduce | flops 256 | bytes 2048
  438.9 12.8 %all_gather.87 = f32[256,256]{1,0:T(8,128)S(1)} all-gather(f32[32,256]{1,0:T(8,128)S(1)} %broadcast_select_fusion.2), channel_id=1, replica_groups=mesh['tm'=64,'state'=8] {'state'}, dimensions={0}, use_global_device_ids=true | all-gather | bytes 294912 | tf_op jit(solution)/shard_map/all_gather | solution.py:69
  458.8 12.8 %all_gather.86 = f32[256,256]{1,0:T(8,128)S(1)} all-gather(f32[32,256]{1,0:T(8,128)S(1)} %add_select_fusion.4), channel_id=1, replica_groups=mesh['tm'=64,'state'=8] {'state'}, dimensions={0}, use_global_device_ids=true | all-gather | bytes 294912 | tf_op jit(solution)/shard_map/all_gather | solution.py:68
  471.8 11.7 %cholesky.484 = f32[128,128]{1,0:T(8,128)S(1)} custom-call(f32[128,128]{1,0:T(8,128)S(1)} %cholesky.660), custom_call_target="Cholesky" | custom-call | tf_op jit(solution)/shard_map/jit(cholesky)/cholesky | solution.py:72
  494.5 11.7 %cholesky.501 = f32[128,128]{1,0:T(8,128)S(1)} custom-call(f32[128,128]{1,0:T(8,128)S(1)} %convolution_subtract_fusion.6), custom_call_target="Cholesky" | custom-call | tf_op jit(solution)/shard_map/jit(cholesky)/cholesky | solution.py:72
  512.5 19.7 %custom-call.60 = f32[2,128,128]{1,2,0:T(8,128)S(1)} custom-call(f32[2,128,128]{2,1,0:T(8,128)S(1)} %get-tuple-element.150), custom_call_target="InvertDiagBlocksLowerTriangular" | custom-call | tf_op jit(solution)/shard_map/jit(_cho_solve)/triangular_solve | solution.py:14
  559.9 13.2 %all-reduce.6 = f32[256]{0:T(256)} all-reduce(f32[256]{0:T(256)S(1)} %get-tuple-element.331), channel_id=1, replica_groups=mesh['tm'=64,'state'=8] {'state'}, use_global_device_ids=true, to_apply=%add.6 | all-reduce | flops 256 | bytes 2048
  573.2 12.8 %all_gather.89 = f32[256,256]{1,0:T(8,128)S(1)} all-gather(f32[32,256]{1,0:T(8,128)S(1)} %broadcast_select_fusion.3), channel_id=1, replica_groups=mesh['tm'=64,'state'=8] {'state'}, dimensions={0}, use_global_device_ids=true | all-gather | bytes 294912 | tf_op jit(solution)/shard_map/all_gather | solution.py:69
  590.3 12.8 %all_gather.88 = f32[256,256]{1,0:T(8,128)S(1)} all-gather(f32[32,256]{1,0:T(8,128)S(1)} %add_select_fusion.3), channel_id=1, replica_groups=mesh['tm'=64,'state'=8] {'state'}, dimensions={0}, use_global_device_ids=true | all-gather | bytes 294912 | tf_op jit(solution)/shard_map/all_gather | solution.py:68
  626.1 11.7 %cholesky.535 = f32[128,128]{1,0:T(8,128)S(1)} custom-call(f32[128,128]{1,0:T(8,128)S(1)} %convolution_subtract_fusion.5), custom_call_target="Cholesky" | custom-call | tf_op jit(solution)/shard_map/jit(cholesky)/cholesky | solution.py:72
  644.9 19.7 %custom-call.63 = f32[2,128,128]{1,2,0:T(8,128)S(1)} custom-call(f32[2,128,128]{2,1,0:T(8,128)S(1)} %get-tuple-element.152), custom_call_target="InvertDiagBlocksLowerTriangular" | custom-call | tf_op jit(solution)/shard_map/jit(_cho_solve)/triangular_solve | solution.py:14
  684.2 13.0 %all-reduce.7 = f32[256]{0:T(256)} all-reduce(f32[256]{0:T(256)S(1)} %get-tuple-element.329), channel_id=1, replica_groups=mesh['tm'=64,'state'=8] {'state'}, use_global_device_ids=true, to_apply=%add.7 | all-reduce | flops 256 | bytes 2048
  697.2 12.8 %all_gather.91 = f32[256,256]{1,0:T(8,128)S(1)} all-gather(f32[32,256]{1,0:T(8,128)S(1)} %broadcast_select_fusion.4), channel_id=1, replica_groups=mesh['tm'=64,'state'=8] {'state'}, dimensions={0}, use_global_device_ids=true | all-gather | bytes 294912 | tf_op jit(solution)/shard_map/all_gather | solution.py:69
  714.4 12.8 %all_gather.90 = f32[256,256]{1,0:T(8,128)S(1)} all-gather(f32[32,256]{1,0:T(8,128)S(1)} %add_select_fusion.2), channel_id=1, replica_groups=mesh['tm'=64,'state'=8] {'state'}, dimensions={0}, use_global_device_ids=true | all-gather | bytes 294912 | tf_op jit(solution)/shard_map/all_gather | solution.py:68
  750.2 11.7 %cholesky.569 = f32[128,128]{1,0:T(8,128)S(1)} custom-call(f32[128,128]{1,0:T(8,128)S(1)} %convolution_subtract_fusion.4), custom_call_target="Cholesky" | custom-call | tf_op jit(solution)/shard_map/jit(cholesky)/cholesky | solution.py:72
  769.4 19.7 %custom-call.66 = f32[2,128,128]{1,2,0:T(8,128)S(1)} custom-call(f32[2,128,128]{2,1,0:T(8,128)S(1)} %get-tuple-element.154), custom_call_target="InvertDiagBlocksLowerTriangular" | custom-call | tf_op jit(solution)/shard_map/jit(_cho_solve)/triangular_solve | solution.py:14
  808.9 12.9 %all-reduce.8 = f32[256]{0:T(256)} all-reduce(f32[256]{0:T(256)S(1)} %get-tuple-element.327), channel_id=1, replica_groups=mesh['tm'=64,'state'=8] {'state'}, use_global_device_ids=true, to_apply=%add.8 | all-reduce | flops 256 | bytes 2048
  821.9 12.8 %all_gather.101 = f32[256,256]{1,0:T(8,128)S(1)} all-gather(f32[32,256]{1,0:T(8,128)S(1)} %broadcast_select_fusion.5), channel_id=1, replica_groups=mesh['tm'=64,'state'=8] {'state'}, dimensions={0}, use_global_device_ids=true | all-gather | bytes 294912 | tf_op jit(solution)/shard_map/all_gather | solution.py:69
  844.7 12.8 %all_gather.92 = f32[256,256]{1,0:T(8,128)S(1)} all-gather(f32[32,256]{1,0:T(8,128)S(1)} %add_select_fusion.1), channel_id=1, replica_groups=mesh['tm'=64,'state'=8] {'state'}, dimensions={0}, use_global_device_ids=true | all-gather | bytes 294912 | tf_op jit(solution)/shard_map/all_gather | solution.py:68
  881.5 11.7 %cholesky.603 = f32[128,128]{1,0:T(8,128)S(1)} custom-call(f32[128,128]{1,0:T(8,128)S(1)} %convolution_subtract_fusion.3), custom_call_target="Cholesky" | custom-call | tf_op jit(solution)/shard_map/jit(cholesky)/cholesky | solution.py:72
  900.2 19.7 %custom-call.70 = f32[2,128,128]{1,2,0:T(8,128)S(1)} custom-call(f32[2,128,128]{2,1,0:T(8,128)S(1)} %get-tuple-element.157), custom_call_target="InvertDiagBlocksLowerTriangular" | custom-call | tf_op jit(solution)/shard_map/jit(_cho_solve)/triangular_solve | solution.py:14
  926.2 19.7 %custom-call.79 = f32[2,128,128]{1,2,0:T(8,128)S(1)} custom-call(f32[2,128,128]{2,1,0:T(8,128)S(1)} %get-tuple-element.165), custom_call_target="InvertDiagBlocksLowerTriangular" | custom-call | tf_op jit(solution)/shard_map/jit(_cho_solve)/triangular_solve | solution.py:14
  961.8 12.4 %all-reduce.9 = f32[256]{0:T(256)S(1)} all-reduce(f32[256]{0:T(256)S(1)} %fusion.296), channel_id=1, replica_groups=mesh['tm'=64,'state'=8] {'state'}, use_global_device_ids=true, to_apply=%add.9 | all-reduce | flops 256 | bytes 2048
  974.2 13.2 %all_gather.102 = f32[256,256]{1,0:T(8,128)S(1)} all-gather(f32[32,256]{1,0:T(8,128)S(1)} %add_select_fusion), channel_id=1, replica_groups=mesh['tm'=64,'state'=8] {'state'}, dimensions={0}, use_global_device_ids=true | all-gather | bytes 294912 | tf_op jit(solution)/shard_map/all_gather | solution.py:93
  1010.4 11.7 %cholesky.637 = f32[128,128]{1,0:T(8,128)S(1)} custom-call(f32[128,128]{1,0:T(8,128)S(1)} %convolution_subtract_fusion.2), custom_call_target="Cholesky" | custom-call | tf_op jit(solution)/shard_map/jit(cholesky)/cholesky | solution.py:96
  1028.3 19.7 %custom-call.73 = f32[2,128,128]{1,2,0:T(8,128)S(1)} custom-call(f32[2,128,128]{2,1,0:T(8,128)S(1)} %get-tuple-element.159), custom_call_target="InvertDiagBlocksLowerTriangular" | custom-call | tf_op jit(solution)/shard_map/jit(_cho_solve)/triangular_solve | solution.py:14
  (644 shorter events, 508.5 us)
Async XLA Ops:
  0.6 947.9 %collective-permute-start.38 = (f32[256]{0:T(256)}, f32[256]{0:T(256)}, u32[]{:S(2)}, u32[]{:S(2)}) collective-permute-start(f32[256]{0:T(256)} %broadcast.237), channel_id=1, source_target_pairs={{0,256},{8,264},{16,272},{24,280},{32,288},{40,296},{48,304},{56,3... | collective-permute-start | bytes 3080 | tf_op jit(solution)/shard_map/ppermute | solution.py:10
  116.4 49.3 %collective-permute-start.20 = (f32[32]{0:T(128)S(1)}, f32[32]{0:T(128)S(1)}, u32[]{:S(2)}, u32[]{:S(2)}) collective-permute-start(f32[32]{0:T(128)S(1)} %dynamic_slice.71), channel_id=1, source_target_pairs={{0,8},{8,16},{16,24},{24,32},{32,40},{40,48},{48,56},{56,64},{64,7... | collective-permute-start | bytes 392 | tf_op jit(solution)/shard_map/ppermute | solution.py:10
  134.4 44.3 %collective-permute-start = (f32[32,256]{1,0:T(8,128)S(1)}, f32[32,256]{1,0:T(8,128)S(1)}, u32[]{:S(2)}, u32[]{:S(2)}) collective-permute-start(f32[32,256]{1,0:T(8,128)S(1)} %dynamic-slice_subtract_fusion), channel_id=1, source_target_pairs={{0,8},{8,16},{16,24},{24,32},{32,40},{40,48},{48,56},{56,64},{64,7... | collective-permute-start | bytes 98312 | tf_op jit(solution)/shard_map/ppermute | solution.py:10
  149.8 111.0 %collective-permute-start.1 = (f32[256,256]{1,0:T(8,128)S(1)}, f32[256,256]{1,0:T(8,128)S(1)}, u32[]{:S(2)}, u32[]{:S(2)}) collective-permute-start(f32[256,256]{1,0:T(8,128)S(1)} %all_gather.83), channel_id=1, source_target_pairs={{0,8},{8,16},{16,24},{24,32},{32,40},{40,48},{48,56},{56,64},{64,7... | collective-permute-start | bytes 786440 | tf_op jit(solution)/shard_map/ppermute | solution.py:10
  253.9 26.7 %collective-permute-start.22 = (f32[32]{0:T(128)S(1)}, f32[32]{0:T(128)S(1)}, u32[]{:S(2)}, u32[]{:S(2)}) collective-permute-start(f32[32]{0:T(128)S(1)} %fusion.43), channel_id=1, source_target_pairs={{0,8},{8,16},{16,24},{24,32},{32,40},{40,48},{48,56},{56,64},{64,7... | collective-permute-start | bytes 392 | tf_op jit(solution)/shard_map/ppermute | solution.py:10
  256.1 74.2 %collective-permute-start.3 = (f32[32,256]{1,0:T(8,128)S(1)}, f32[32,256]{1,0:T(8,128)S(1)}, u32[]{:S(2)}, u32[]{:S(2)}) collective-permute-start(f32[32,256]{1,0:T(8,128)S(1)} %convolution_multiply_fusion.5), channel_id=1, source_target_pairs={{0,8},{8,16},{16,24},{24,32},{32,40},{40,48},{48,56},{56,64},{64,7... | collective-permute-start | bytes 98312 | tf_op jit(solution)/shard_map/ppermute | solution.py:10
  262.5 34.1 %collective-permute-start.21 = (f32[32]{0:T(128)S(1)}, f32[32]{0:T(128)S(1)}, u32[]{:S(2)}, u32[]{:S(2)}) collective-permute-start(f32[32]{0:T(128)S(1)} %fusion.42), channel_id=1, source_target_pairs={{8,0},{16,8},{24,16},{32,24},{40,32},{48,40},{56,48},{64,56},{72,6... | collective-permute-start | bytes 392 | tf_op jit(solution)/shard_map/ppermute | solution.py:10
  277.3 53.0 %collective-permute-start.2 = (f32[32,256]{1,0:T(8,128)S(1)}, f32[32,256]{1,0:T(8,128)S(1)}, u32[]{:S(2)}, u32[]{:S(2)}) collective-permute-start(f32[32,256]{1,0:T(8,128)S(1)} %fusion.10), channel_id=1, source_target_pairs={{8,0},{16,8},{24,16},{32,24},{40,32},{48,40},{56,48},{64,56},{72,6... | collective-permute-start | bytes 98312 | tf_op jit(solution)/shard_map/ppermute | solution.py:10
  280.7 31.0 %collective-permute-start.4 = (f32[32,256]{1,0:T(8,128)S(1)}, f32[32,256]{1,0:T(8,128)S(1)}, u32[]{:S(2)}, u32[]{:S(2)}) collective-permute-start(f32[32,256]{1,0:T(8,128)S(1)} %fusion.9), channel_id=1, source_target_pairs={{8,0},{16,8},{24,16},{32,24},{40,32},{48,40},{56,48},{64,56},{72,6... | collective-permute-start | bytes 98312 | tf_op jit(solution)/shard_map/ppermute | solution.py:10
  324.6 90.2 %collective-permute-start.5 = (f32[256,256]{1,0:T(8,128)S(1)}, f32[256,256]{1,0:T(8,128)S(1)}, u32[]{:S(2)}, u32[]{:S(2)}) collective-permute-start(f32[256,256]{1,0:T(8,128)S(1)} %all_gather.85), channel_id=1, source_target_pairs={{0,16},{8,24},{16,32},{24,40},{32,48},{40,56},{48,64},{56,72},{64,... | collective-permute-start | bytes 786440 | tf_op jit(solution)/shard_map/ppermute | solution.py:10
  405.4 17.0 %collective-permute-start.24 = (f32[32]{0:T(128)S(1)}, f32[32]{0:T(128)S(1)}, u32[]{:S(2)}, u32[]{:S(2)}) collective-permute-start(f32[32]{0:T(128)S(1)} %fusion.44), channel_id=1, source_target_pairs={{0,16},{8,24},{16,32},{24,40},{32,48},{40,56},{48,64},{56,72},{64,... | collective-permute-start | bytes 392 | tf_op jit(solution)/shard_map/ppermute | solution.py:10
  410.1 48.7 %collective-permute-start.7 = (f32[32,256]{1,0:T(8,128)S(1)}, f32[32,256]{1,0:T(8,128)S(1)}, u32[]{:S(2)}, u32[]{:S(2)}) collective-permute-start(f32[32,256]{1,0:T(8,128)S(1)} %convolution_multiply_fusion.4), channel_id=1, source_target_pairs={{0,16},{8,24},{16,32},{24,40},{32,48},{40,56},{48,64},{56,72},{64,... | collective-permute-start | bytes 98312 | tf_op jit(solution)/shard_map/ppermute | solution.py:10
  416.4 9.7 collective-permute-start.23
  418.8 39.9 %collective-permute-start.6 = (f32[32,256]{1,0:T(8,128)S(1)}, f32[32,256]{1,0:T(8,128)S(1)}, u32[]{:S(2)}, u32[]{:S(2)}) collective-permute-start(f32[32,256]{1,0:T(8,128)S(1)} %fusion.8), channel_id=1, source_target_pairs={{16,0},{24,8},{32,16},{40,24},{48,32},{56,40},{64,48},{72,56},{80,... | collective-permute-start | bytes 98312 | tf_op jit(solution)/shard_map/ppermute | solution.py:10
  422.4 16.5 %collective-permute-start.8 = (f32[32,256]{1,0:T(8,128)S(1)}, f32[32,256]{1,0:T(8,128)S(1)}, u32[]{:S(2)}, u32[]{:S(2)}) collective-permute-start(f32[32,256]{1,0:T(8,128)S(1)} %fusion.7), channel_id=1, source_target_pairs={{16,0},{24,8},{32,16},{40,24},{48,32},{56,40},{64,48},{72,56},{80,... | collective-permute-start | bytes 98312 | tf_op jit(solution)/shard_map/ppermute | solution.py:10
  451.8 91.2 %collective-permute-start.9 = (f32[256,256]{1,0:T(8,128)S(1)}, f32[256,256]{1,0:T(8,128)S(1)}, u32[]{:S(2)}, u32[]{:S(2)}) collective-permute-start(f32[256,256]{1,0:T(8,128)S(1)} %all_gather.87), channel_id=1, source_target_pairs={{0,32},{8,40},{16,48},{24,56},{32,64},{40,72},{48,80},{56,88},{64,... | collective-permute-start | bytes 786440 | tf_op jit(solution)/shard_map/ppermute | solution.py:10
  533.7 22.7 %collective-permute-start.26 = (f32[32]{0:T(128)S(1)}, f32[32]{0:T(128)S(1)}, u32[]{:S(2)}, u32[]{:S(2)}) collective-permute-start(f32[32]{0:T(128)S(1)} %fusion.45), channel_id=1, source_target_pairs={{0,32},{8,40},{16,48},{24,56},{32,64},{40,72},{48,80},{56,88},{64,... | collective-permute-start | bytes 392 | tf_op jit(solution)/shard_map/ppermute | solution.py:10
  536.7 53.0 %collective-permute-start.11 = (f32[32,256]{1,0:T(8,128)S(1)}, f32[32,256]{1,0:T(8,128)S(1)}, u32[]{:S(2)}, u32[]{:S(2)}) collective-permute-start(f32[32,256]{1,0:T(8,128)S(1)} %convolution_multiply_fusion.3), channel_id=1, source_target_pairs={{0,32},{8,40},{16,48},{24,56},{32,64},{40,72},{48,80},{56,88},{64,... | collective-permute-start | bytes 98312 | tf_op jit(solution)/shard_map/ppermute | solution.py:10
  544.7 14.6 %collective-permute-start.25 = (f32[32]{0:T(128)S(1)}, f32[32]{0:T(128)S(1)}, u32[]{:S(2)}, u32[]{:S(2)}) collective-permute-start(f32[32]{0:T(128)S(1)} %fusion.40), channel_id=1, source_target_pairs={{32,0},{40,8},{48,16},{56,24},{64,32},{72,40},{80,48},{88,56},{96,... | collective-permute-start | bytes 392 | tf_op jit(solution)/shard_map/ppermute | solution.py:10
  548.4 41.3 %collective-permute-start.10 = (f32[32,256]{1,0:T(8,128)S(1)}, f32[32,256]{1,0:T(8,128)S(1)}, u32[]{:S(2)}, u32[]{:S(2)}) collective-permute-start(f32[32,256]{1,0:T(8,128)S(1)} %fusion.6), channel_id=1, source_target_pairs={{32,0},{40,8},{48,16},{56,24},{64,32},{72,40},{80,48},{88,56},{96,... | collective-permute-start | bytes 98312 | tf_op jit(solution)/shard_map/ppermute | solution.py:10
  556.4 16.8 %collective-permute-start.12 = (f32[32,256]{1,0:T(8,128)S(1)}, f32[32,256]{1,0:T(8,128)S(1)}, u32[]{:S(2)}, u32[]{:S(2)}) collective-permute-start(f32[32,256]{1,0:T(8,128)S(1)} %fusion.5), channel_id=1, source_target_pairs={{32,0},{40,8},{48,16},{56,24},{64,32},{72,40},{80,48},{88,56},{96,... | collective-permute-start | bytes 98312 | tf_op jit(solution)/shard_map/ppermute | solution.py:10
  586.1 85.6 %collective-permute-start.13 = (f32[256,256]{1,0:T(8,128)S(1)}, f32[256,256]{1,0:T(8,128)S(1)}, u32[]{:S(2)}, u32[]{:S(2)}) collective-permute-start(f32[256,256]{1,0:T(8,128)S(1)} %all_gather.89), channel_id=1, source_target_pairs={{0,64},{8,72},{16,80},{24,88},{32,96},{40,104},{48,112},{56,120},{... | collective-permute-start | bytes 786440 | tf_op jit(solution)/shard_map/ppermute | solution.py:10
  666.7 14.0 %collective-permute-start.28 = (f32[32]{0:T(128)S(1)}, f32[32]{0:T(128)S(1)}, u32[]{:S(2)}, u32[]{:S(2)}) collective-permute-start(f32[32]{0:T(128)S(1)} %fusion.46), channel_id=1, source_target_pairs={{0,64},{8,72},{16,80},{24,88},{32,96},{40,104},{48,112},{56,120},{... | collective-permute-start | bytes 392 | tf_op jit(solution)/shard_map/ppermute | solution.py:10
  668.8 45.5 %collective-permute-start.15 = (f32[32,256]{1,0:T(8,128)S(1)}, f32[32,256]{1,0:T(8,128)S(1)}, u32[]{:S(2)}, u32[]{:S(2)}) collective-permute-start(f32[32,256]{1,0:T(8,128)S(1)} %convolution_multiply_fusion.2), channel_id=1, source_target_pairs={{0,64},{8,72},{16,80},{24,88},{32,96},{40,104},{48,112},{56,120},{... | collective-permute-start | bytes 98312 | tf_op jit(solution)/shard_map/ppermute | solution.py:10
  673.4 9.6 collective-permute-start.27
  676.7 37.7 %collective-permute-start.14 = (f32[32,256]{1,0:T(8,128)S(1)}, f32[32,256]{1,0:T(8,128)S(1)}, u32[]{:S(2)}, u32[]{:S(2)}) collective-permute-start(f32[32,256]{1,0:T(8,128)S(1)} %fusion.4), channel_id=1, source_target_pairs={{64,0},{72,8},{80,16},{88,24},{96,32},{104,40},{112,48},{120,56},{... | collective-permute-start | bytes 98312 | tf_op jit(solution)/shard_map/ppermute | solution.py:10
  680.7 16.5 %collective-permute-start.16 = (f32[32,256]{1,0:T(8,128)S(1)}, f32[32,256]{1,0:T(8,128)S(1)}, u32[]{:S(2)}, u32[]{:S(2)}) collective-permute-start(f32[32,256]{1,0:T(8,128)S(1)} %fusion.3), channel_id=1, source_target_pairs={{64,0},{72,8},{80,16},{88,24},{96,32},{104,40},{112,48},{120,56},{... | collective-permute-start | bytes 98312 | tf_op jit(solution)/shard_map/ppermute | solution.py:10
  710.1 85.2 %collective-permute-start.17 = (f32[256,256]{1,0:T(8,128)S(1)}, f32[256,256]{1,0:T(8,128)}, u32[]{:S(2)}, u32[]{:S(2)}) collective-permute-start(f32[256,256]{1,0:T(8,128)S(1)} %all_gather.91), channel_id=1, source_target_pairs={{0,128},{8,136},{16,144},{24,152},{32,160},{40,168},{48,176},{56,1... | collective-permute-start | bytes 786440 | tf_op jit(solution)/shard_map/ppermute | solution.py:10
  791.2 14.6 %collective-permute-start.30 = (f32[32]{0:T(128)S(1)}, f32[32]{0:T(128)S(1)}, u32[]{:S(2)}, u32[]{:S(2)}) collective-permute-start(f32[32]{0:T(128)S(1)} %fusion.47), channel_id=1, source_target_pairs={{0,128},{8,136},{16,144},{24,152},{32,160},{40,168},{48,176},{56,1... | collective-permute-start | bytes 392 | tf_op jit(solution)/shard_map/ppermute | solution.py:10
  793.4 50.7 %collective-permute-start.19 = (f32[32,256]{1,0:T(8,128)S(1)}, f32[32,256]{1,0:T(8,128)S(1)}, u32[]{:S(2)}, u32[]{:S(2)}) collective-permute-start(f32[32,256]{1,0:T(8,128)S(1)} %convolution_multiply_fusion.1), channel_id=1, source_target_pairs={{0,128},{8,136},{16,144},{24,152},{32,160},{40,168},{48,176},{56,1... | collective-permute-start | bytes 98312 | tf_op jit(solution)/shard_map/ppermute | solution.py:10
  797.7 10.0 collective-permute-start.29
  803.8 40.3 %collective-permute-start.18 = (f32[32,256]{1,0:T(8,128)S(1)}, f32[32,256]{1,0:T(8,128)S(1)}, u32[]{:S(2)}, u32[]{:S(2)}) collective-permute-start(f32[32,256]{1,0:T(8,128)S(1)} %fusion.2), channel_id=1, source_target_pairs={{128,0},{136,8},{144,16},{152,24},{160,32},{168,40},{176,48},{184,... | collective-permute-start | bytes 98312 | tf_op jit(solution)/shard_map/ppermute | solution.py:10
  805.8 16.1 %collective-permute-start.31 = (f32[32,256]{1,0:T(8,128)S(1)}, f32[32,256]{1,0:T(8,128)S(1)}, u32[]{:S(2)}, u32[]{:S(2)}) collective-permute-start(f32[32,256]{1,0:T(8,128)S(1)} %fusion.1), channel_id=1, source_target_pairs={{128,0},{136,8},{144,16},{152,24},{160,32},{168,40},{176,48},{184,... | collective-permute-start | bytes 98312 | tf_op jit(solution)/shard_map/ppermute | solution.py:10
  834.9 114.5 %collective-permute-start.32 = (f32[256,256]{1,0:T(8,128)S(1)}, f32[256,256]{1,0:T(8,128)}, u32[]{:S(2)}, u32[]{:S(2)}) collective-permute-start(f32[256,256]{1,0:T(8,128)S(1)} %all_gather.101), channel_id=1, source_target_pairs={{0,256},{8,264},{16,272},{24,280},{32,288},{40,296},{48,304},{56,3... | collective-permute-start | bytes 786440 | tf_op jit(solution)/shard_map/ppermute | solution.py:10
  945.8 9.7 collective-permute-start.36
  947.1 27.1 %collective-permute-start.34 = (f32[32,256]{1,0:T(8,128)S(1)}, f32[32,256]{1,0:T(8,128)S(1)}, u32[]{:S(2)}, u32[]{:S(2)}) collective-permute-start(f32[32,256]{1,0:T(8,128)S(1)} %convolution_multiply_fusion), channel_id=1, source_target_pairs={{0,256},{8,264},{16,272},{24,280},{32,288},{40,296},{48,304},{56,3... | collective-permute-start | bytes 98312 | tf_op jit(solution)/shard_map/ppermute | solution.py:10
  951.5 9.5 collective-permute-start.35
  954.3 19.9 %collective-permute-start.33 = (f32[32,256]{1,0:T(8,128)S(1)}, f32[32,256]{1,0:T(8,128)S(1)}, u32[]{:S(2)}, u32[]{:S(2)}) collective-permute-start(f32[32,256]{1,0:T(8,128)S(1)} %fusion), channel_id=1, source_target_pairs={{256,0},{264,8},{272,16},{280,24},{288,32},{296,40},{304,48},{312,... | collective-permute-start | bytes 98312 | tf_op jit(solution)/shard_map/ppermute | solution.py:10
  1055.7 9.4 collective-permute-start.40
  1057.0 11.0 collective-permute-start.39
  1074.8 9.5 collective-permute-start.42
  1088.9 11.8 %collective-permute-start.46 = (f32[256]{0:T(256)S(1)}, f32[256]{0:T(256)S(1)}, u32[]{:S(2)}, u32[]{:S(2)}) collective-permute-start(f32[256]{0:T(256)S(1)} %broadcast_select_fusion.10), channel_id=1, source_target_pairs={{64,0},{72,8},{80,16},{88,24},{96,32},{104,40},{112,48},{120,56},{... | collective-permute-start | bytes 3080 | tf_op jit(solution)/shard_map/ppermute | solution.py:10
  1091.8 11.4 collective-permute-start.45
  1100.7 9.4 collective-permute-start.47
  1111.6 11.5 collective-permute-start.49
  1114.5 13.5 %collective-permute-start.48 = (f32[256]{0:T(256)S(1)}, f32[256]{0:T(256)S(1)}, u32[]{:S(2)}, u32[]{:S(2)}) collective-permute-start(f32[256]{0:T(256)S(1)} %broadcast_select_fusion.9), channel_id=1, source_target_pairs={{0,16},{8,24},{16,32},{24,40},{32,48},{40,56},{48,64},{56,72},{64,... | collective-permute-start | bytes 3080 | tf_op jit(solution)/shard_map/ppermute | solution.py:10
  1130.9 10.2 collective-permute-start.52
  1135.7 9.9 collective-permute-start.51
  (53 other events, 700.8 us)
where the time goes:
time: 1170 us; the launch traced here: 1160 us
  other arithmetic  458 us (39%)
  blocking collectives  326 us (28%)
  starting transfers between devices  228 us (19%)
  local copies, waits for them, and re-layouts  53.4 us (5%)
  matrix products  46.8 us (4%)
  waiting for transfers between devices  31.5 us (3%)
  between operations  14.1 us (1%)
    ppermute x55, starting transfers between devices, from_behind(): return lax.ppermute(shard, axis, pairs)  228 us
    another operation x42, other arithmetic, body(): factor = jnp.linalg.cholesky(full_a)  208 us
    another operation x26, other arithmetic, solve_with(): return jax.scipy.linalg.cho_solve((factor, True), right_side)  177 us
    unnamed x7, blocking collectives  91.8 us
    all_gather x7, blocking collectives, body(): lax.all_gather(block_a, 'state', axis=0, tiled=True)  90.6 us
    all_gather x6, blocking collectives, body(): lax.all_gather(block_c, 'state', axis=0, tiled=True)  77 us
    another operation x7, other arithmetic, body(): root_x = solve_with(jnp.linalg.cholesky(root_a), root_h)  34.6 us
    another operation x6, other arithmetic, body(): factor = jnp.linalg.cholesky(whole_a)  34 us
  transfers between devices with their start and end apart: 55, of which 11 were waited for; matrix products, arithmetic and copies ran while one was open for 41% of the time, Pallas kernels for 0%

commit v1 on v0

v1 whole, which is shorter than its diff:
```python
import jax
import jax.numpy as jnp
from jax import lax
from jax.experimental import pallas as pl
from jax.experimental.pallas import tpu as pltpu
from jax.sharding import PartitionSpec as P

N = 256
H = 128
F32 = jnp.float32
MESH = pl.DeviceIdType.MESH
EXACT = lax.Precision.HIGHEST


def nt(a, b):
    return lax.dot_general(
        a, b, (((1,), (1,)), ((), ())), precision=EXACT, preferred_element_type=F32
    )


def nn(a, b):
    return jnp.dot(a, b, precision=EXACT, preferred_element_type=F32)


def row_of(x, k):
    return jnp.broadcast_to(x[k : k + 1, :], x.shape)


def lane_of(x, l):
    return jnp.broadcast_to(x[:, l : l + 1], (x.shape[0], H))


def sum8(t):
    return ((t[0] + t[1]) + (t[2] + t[3])) + ((t[4] + t[5]) + (t[6] + t[7]))


def invert8(columns, sub):
    c = list(columns)
    factor_rows = []
    for k in range(8):
        row = [row_of(c[j], k) for j in range(8)]
        inverse = 1.0 / row[k]
        root = lax.rsqrt(row[k])
        factor_rows.append([row[j] * root for j in range(k)] + [root])
        pivot_column = c[k]
        at = sub == k
        for j in range(8):
            if j != k:
                t = row[j] * inverse
                c[j] = jnp.where(at, t, c[j] - pivot_column * t)
        c[k] = jnp.where(at, inverse, -pivot_column * inverse)
    return c, factor_rows


def inverse_factor(a):
    w = [a[8 * r : 8 * r + 8, :] for r in range(16)]
    sub = lax.broadcasted_iota(jnp.int32, (8, H), 0)
    lane = lax.broadcasted_iota(jnp.int32, (8, H), 1)
    out = []
    for b in range(16):
        at = 8 * b
        inverse, factor_rows = invert8([lane_of(w[b], at + j) for j in range(8)], sub)
        inside = (lane >= at) & (lane < at + 8)
        panel = jnp.where(inside, (lane - at == sub).astype(F32), w[b])
        rows = [row_of(panel, j) for j in range(8)]
        scaled = sum8([inverse[j] * rows[j] for j in range(8)])
        done = []
        for j in range(8):
            column = jnp.zeros((8, H), F32)
            for i in range(j, 8):
                column = jnp.where(sub == i, factor_rows[i][j], column)
            done.append(column * rows[j])
        out.append(jnp.where(lane < at + 8, sum8(done), 0.0))
        if b < 15:
            scaled_rows = [row_of(scaled, j) for j in range(8)]
            for i in range(b + 1, 16):
                cols = [lane_of(w[i], at + j) for j in range(8)]
                w[i] = jnp.where(inside, 0.0, w[i]) - sum8(
                    [cols[j] * scaled_rows[j] for j in range(8)]
                )
    return jnp.concatenate(out, axis=0)


def eliminate(block, x, v, f1, f2, z):
    f1[...] = inverse_factor(block[0:H, 0:H])
    z[...] = nt(block[H:N, 0:H], f1[...])
    v[:, 0:H] = nt(x[:, 0:H], f1[...])
    f2[...] = inverse_factor(block[H:N, H:N] - nt(z[...], z[...]))
    y = x[:, H:N] - nt(v[:, 0:H], z[...])
    v[:, H:N] = nt(y, f2[...])


def means(v, f1, f2, z):
    hi = nn(v[:, H:N], f2[...])
    lo = nn(v[:, 0:H] - nn(hi, z[...]), f1[...])
    return lo, hi


def kernel(
    diag, coup, info, out,
    d1, c0, c1, hin, d2, xl, xu, xcat, v1, v2, f1a, f2a, za, f1b, f2b, zb, ga, gb,
    own_d, own_h, rc, rxl, rxu, su0, sx0, sl, su, sx, xin, xown,
    g1_send, g1_recv, g2_send, g2_recv, rc_recv, rx_recv, s_send, x_send, x_recv,
):
    s = lax.axis_index("tm")
    j = lax.axis_index("state")
    rows = pl.ds(pl.multiple_of(j * 32, 32), 32)

    def divides(d):
        return lax.rem(s, d) == 0

    barrier = pltpu.get_barrier_semaphore()
    count = jnp.int32(7)
    for r in range(1, 8):
        pl.semaphore_signal(
            barrier, inc=1, device_id=(s, lax.rem(j + r, 8)), device_id_type=MESH
        )
    for k in range(6):
        d = 2**k
        down = divides(d) & (s >= d)
        up = divides(d) & (s + d < 64)
        count = count + down.astype(jnp.int32) + up.astype(jnp.int32)

        @pl.when(down)
        def _():
            pl.semaphore_signal(barrier, inc=1, device_id=(s - d, j), device_id_type=MESH)

        @pl.when(up)
        def _():
            pl.semaphore_signal(barrier, inc=1, device_id=(s + d, j), device_id_type=MESH)

    pl.semaphore_wait(barrier, count)

    def to(src, dst, send, recv, tm, state):
        return pltpu.make_async_remote_copy(
            src_ref=src, dst_ref=dst, send_sem=send, recv_sem=recv,
            device_id=(tm, state), device_id_type=MESH,
        )

    def peer(src, dst, sends, recvs, a, r):
        return to(src, dst, sends.at[a, r], recvs.at[a, r], s, lax.rem(j + r, 8))

    first = [
        (diag.at[1], d1.at[rows]),
        (coup.at[0], c0.at[rows]),
        (coup.at[1], c1.at[rows]),
        (info, hin.at[pl.ds(pl.multiple_of(j * 8, 8), 8)]),
    ]
    for a, (src, dst) in enumerate(first):
        for r in range(1, 8):
            peer(src, dst, g1_send, g1_recv, a, r).start()
    for src, dst in first:
        dst[...] = src[...]
    for a, (src, dst) in enumerate(first):
        for r in range(1, 8):
            peer(src, dst, g1_send, g1_recv, a, r).wait_recv()

    info_all = sum8([hin[8 * i : 8 * i + 8, :] for i in range(8)])
    xcat[0:N, :] = c0[...]
    xcat[N : 2 * N, :] = jnp.where(s == 63, 0.0, c1[...].T)
    xcat[2 * N : 2 * N + 8, :] = row_of(info_all, 1)
    eliminate(d1, xcat, v1, f1a, f2a, za)

    def gram(v):
        start = pl.multiple_of(j * 32, 32)
        left = jnp.concatenate(
            [v[pl.ds(start, 32), :], v[pl.ds(start + N, 32), :], v[2 * N : 2 * N + 8, :]], axis=0
        )
        return nt(left, v[0 : 2 * N, :])

    prod = gram(v1)
    su0[0:32, :] = prod[32:64, N : 2 * N]
    su0[32:40, :] = prod[64:72, N : 2 * N]
    sx0[...] = -prod[0:32, N : 2 * N]
    rxu_local = -prod[32:64, 0:N]
    own_d[...] = diag[0] - prod[0:32, 0:N]
    own_h[...] = row_of(info_all, 0) - prod[64:72, 0:N]
    up0 = s < 63
    even = divides(2)

    def send_up0():
        return to(su0, rc.at[0], s_send.at[0], rc_recv.at[0], s + 1, j)

    def send_x0():
        return to(sx0, rxl, s_send.at[1], rx_recv.at[0], s + 1, j)

    @pl.when(up0)
    def _():
        send_up0().start()

    @pl.when(even)
    def _():
        send_x0().start()

    def take(slot, tm):
        to(sl, rc.at[slot], s_send.at[2], rc_recv.at[slot], tm, j).wait_recv()
        own_d[...] = own_d[...] - rc[slot, 0:32, :]
        own_h[...] = own_h[...] - rc[slot, 32:40, :]

    @pl.when(s > 0)
    def _():
        take(0, s - 1)

    for k in range(6):
        d = 2**k

        @pl.when(divides(2 * d) & (s > 0))
        def _():
            take(1 + 2 * k, s - d)

        @pl.when(divides(2 * d))
        def _():
            take(2 + 2 * k, s + d)

    def each_peer(src, dst, a, act):
        for r in range(1, 8):
            act(peer(src, dst, g2_send, g2_recv, a, r))

    each_peer(own_d, d2.at[rows], 0, lambda c: c.start())
    d2[rows, :] = own_d[...]

    @pl.when(s > 0)
    def _():
        to(sx0, rxl, s_send.at[1], rx_recv.at[0], s - 1, j).wait_recv()
        each_peer(rxl, xl.at[rows], 1, lambda c: c.start())
        xl[rows, :] = rxl[...]

        @pl.when(even)
        def _():
            to(sx, rxu, s_send.at[4], rx_recv.at[1], s - 1, j).wait_recv()

        @pl.when(jnp.logical_not(even))
        def _():
            rxu[...] = rxu_local

        each_peer(rxu, xu.at[rows], 2, lambda c: c.start())
        xu[rows, :] = rxu[...]

    each_peer(own_d, d2.at[rows], 0, lambda c: c.wait_recv())

    @pl.when(s > 0)
    def _():
        each_peer(rxl, xl.at[rows], 1, lambda c: c.wait_recv())
        each_peer(rxu, xu.at[rows], 2, lambda c: c.wait_recv())
        xcat[0:N, :] = xl[...]
        xcat[N : 2 * N, :] = xu[...]

    @pl.when(s == 0)
    def _():
        xcat[0 : 2 * N, :] = jnp.zeros((2 * N, N), F32)

    xcat[2 * N : 2 * N + 8, :] = own_h[...]
    eliminate(d2, xcat, v2, f1b, f2b, zb)
    prod = gram(v2)
    sl[0:32, :] = prod[0:32, 0:N]
    sl[32:40, :] = prod[64:72, 0:N]
    su[0:32, :] = prod[32:64, N : 2 * N]
    su[32:40, :] = prod[64:72, N : 2 * N]

    own_level = []
    for k in range(6):
        d = 2**k
        mine = lax.rem(s, 2 * d) == d
        own_level.append((k, d, mine))

    def sends(act):
        for k, d, mine in own_level:

            @pl.when(mine)
            def _():
                act(to(sl, rc.at[2 + 2 * k], s_send.at[2], rc_recv.at[2 + 2 * k], s - d, j))

            @pl.when(mine & (s + d < 64))
            def _():
                act(to(su, rc.at[1 + 2 * k], s_send.at[3], rc_recv.at[1 + 2 * k], s + d, j))

    def x_sends(act):
        for k, d, mine in own_level:
            if k == 5:
                continue

            @pl.when(mine & (lax.rem(s - d, 4 * d) == 2 * d))
            def _():
                act(to(sx, rxu, s_send.at[4], rx_recv.at[1], s - d, j))

            @pl.when(mine & (s + d < 64) & (lax.rem(s + d, 4 * d) == 2 * d))
            def _():
                act(to(sx, rxl, s_send.at[4], rx_recv.at[0], s + d, j))

    sends(lambda c: c.start())
    to_lower = jnp.bool_(False)
    for k, d, mine in own_level:
        to_lower = to_lower | (mine & (lax.rem(s - d, 4 * d) == 2 * d))

    @pl.when(to_lower)
    def _():
        sx[...] = -prod[32:64, 0:N]

    @pl.when(jnp.logical_not(to_lower))
    def _():
        sx[...] = -prod[0:32, N : 2 * N]

    x_sends(lambda c: c.start())

    lo, hi = means(v2, f1b, f2b, zb)
    gb[:, 0:H] = lo
    gb[:, H:N] = hi

    for k, d, mine in own_level:

        @pl.when(mine)
        def _():
            to(xown, xin.at[0], x_send.at[0], x_recv.at[0], s - d, j).wait_recv()

        @pl.when(mine & (s + d < 64))
        def _():
            to(xown, xin.at[1], x_send.at[0], x_recv.at[1], s + d, j).wait_recv()

        @pl.when(mine & (s + d >= 64))
        def _():
            xin[1] = jnp.zeros((8, N), F32)

    @pl.when(s == 0)
    def _():
        xown[...] = gb[2 * N : 2 * N + 8, :]

    @pl.when(s > 0)
    def _():
        xown[...] = gb[2 * N : 2 * N + 8, :] - (
            nn(xin[0], gb[0:N, :]) + nn(xin[1], gb[N : 2 * N, :])
        )

    def spread(act):
        for k in reversed(range(6)):
            d = 2**k

            @pl.when(divides(2 * d))
            def _():
                act(to(xown, xin.at[0], x_send.at[2 * k], x_recv.at[0], s + d, j))

            @pl.when(divides(2 * d) & (s > 0))
            def _():
                act(to(xown, xin.at[1], x_send.at[2 * k + 1], x_recv.at[1], s - d, j))

        @pl.when(jnp.logical_not(even))
        def _():
            act(to(xown, xin.at[2], x_send.at[12], x_recv.at[2], s - 1, j))

    spread(lambda c: c.start())

    lo, hi = means(v1, f1a, f2a, za)
    ga[:, 0:H] = lo
    ga[:, H:N] = hi
    part = ga[2 * N : 2 * N + 8, :] - nn(xown[...], ga[0:N, :])

    @pl.when(even)
    def _():
        to(xown, xin.at[2], x_send.at[12], x_recv.at[2], s + 1, j).wait_recv()

    @pl.when(jnp.logical_not(even))
    def _():
        xin[2] = xin[1]

    later = part - nn(xin[2], ga[N : 2 * N, :])
    both = jnp.concatenate([xown[0:1, :], later[0:1, :]], axis=0)
    for i in range(8):

        @pl.when(j == i)
        def _():
            out[...] = both[:, 32 * i : 32 * i + 32]

    for a, (src, dst) in enumerate(first):
        for r in range(1, 8):
            peer(src, dst, g1_send, g1_recv, a, r).wait_send()

    @pl.when(up0)
    def _():
        send_up0().wait_send()

    @pl.when(even)
    def _():
        send_x0().wait_send()

    each_peer(own_d, d2.at[rows], 0, lambda c: c.wait_send())

    @pl.when(s > 0)
    def _():
        each_peer(rxl, xl.at[rows], 1, lambda c: c.wait_send())
        each_peer(rxu, xu.at[rows], 2, lambda c: c.wait_send())

    sends(lambda c: c.wait_send())
    x_sends(lambda c: c.wait_send())
    spread(lambda c: c.wait_send())


def body(diagonal, coupling, info):
    offset = lax.axis_index("state") * 32
    placed = lax.dynamic_update_slice(jnp.zeros((8, N), F32), info, (0, offset))
    vmem = pltpu.VMEM
    dma = pltpu.SemaphoreType.DMA
    square = vmem((N, N), F32)
    half = vmem((H, H), F32)
    tall = vmem((2 * N + 8, N), F32)
    return pl.pallas_call(
        kernel,
        out_shape=jax.ShapeDtypeStruct((2, 32), F32),
        in_specs=[pl.BlockSpec(memory_space=vmem)] * 3,
        out_specs=pl.BlockSpec(memory_space=vmem),
        scratch_shapes=[
            square, square, square, vmem((64, N), F32), square, square, square, tall, tall, tall,
            half, half, half, half, half, half, tall, tall,
            vmem((32, N), F32), vmem((8, N), F32), vmem((13, 40, N), F32),
            vmem((32, N), F32), vmem((32, N), F32),
            vmem((40, N), F32), vmem((32, N), F32),
            vmem((40, N), F32), vmem((40, N), F32), vmem((32, N), F32),
            vmem((3, 8, N), F32), vmem((8, N), F32),
            dma((4, 8)), dma((4, 8)), dma((3, 8)), dma((3, 8)),
            dma((13,)), dma((2,)), dma((5,)), dma((13,)), dma((3,)),
        ],
        compiler_params=pltpu.CompilerParams(
            collective_id=0, has_side_effects=True, vmem_limit_bytes=32 * 1024 * 1024
        ),
    )(diagonal, coupling, placed)


def solution(mesh):
    placed = (P("tm", "state", None), P("tm", "state", None), P("tm", "state"))
    return jax.shard_map(
        body, mesh=mesh, in_specs=placed, out_specs=P("tm", "state"), check_vma=False
    )
```

time: 1170 us -> 252 us (0.22)
  the two profiles are of different devices: /device:TPU:248 before, /device:TPU:8 now
where the time goes in v1:
time: 252 us
  Pallas kernels  248 us (98%)
  local copies, waits for them, and re-layouts  3.15 us (1%)
    pallas_call x1, Pallas kernels, body(): pl.pallas_call(kernel, out_shape=jax.ShapeDtypeStruct((2, 32), F32), in_s...  248 us

profile of v1, /device:TPU:8, one launch (start us, length us, event | category | flops | bytes accessed | tf_op | source)
XLA Modules:
  0.0 251.6 jit_solution(17448394228550825718)
XLA Ops:
  0.0 0.0 copy-start.2
  0.0 0.7 copy-done.2
  0.7 0.2 dynamic_update_slice.3.info
  0.9 0.0 copy-start
  0.9 0.8 copy-done
  1.8 0.0 copy-start.1
  1.8 0.8 copy-done.1
  2.6 248.4 %shard_map.37 = f32[2,32]{1,0:T(2,128)S(1)} custom-call(f32[2,32,256]{2,1,0:T(8,128)S(1)} %copy-done, f32[2,32,256]{2,1,0:T(8,128)S(1)} %copy-done.1, f32[8,256]{1,0:T(8,128)S(1)} %dynamic_update_slice.3.info), custom_call_target="tpu_custom_call" | custom-call | tf_op jit(solution)/shard_map/pallas_call | solution.py:404
  251.0 0.6 copy.6
  (1 shorter events, 0.0 us)
Async XLA Ops:
  0.0 0.7 copy-start.2
  0.9 0.8 copy-start
  1.8 0.8 copy-start.1

commit v2 on v1

v2 whole, which is shorter than its diff:
```python
import jax
import jax.numpy as jnp
from jax import lax
from jax.experimental import pallas as pl
from jax.experimental.pallas import tpu as pltpu
from jax.sharding import PartitionSpec as P

N = 256
H = 128
F32 = jnp.float32
MESH = pl.DeviceIdType.MESH
EXACT = lax.Precision.HIGHEST


def nt(a, b):
    return lax.dot_general(
        a, b, (((1,), (1,)), ((), ())), precision=EXACT, preferred_element_type=F32
    )


def nn(a, b):
    return jnp.dot(a, b, precision=EXACT, preferred_element_type=F32)


def row_of(x, k):
    return jnp.broadcast_to(x[k : k + 1, :], x.shape)


def lane_of(x, l):
    return jnp.take_along_axis(x, jnp.full((8, H), l, jnp.int32), axis=1)


def sum8(t):
    return ((t[0] + t[1]) + (t[2] + t[3])) + ((t[4] + t[5]) + (t[6] + t[7]))


def pivot_block(w, b, sub, lane):
    at = 8 * b
    c = [lane_of(w[b], at + j) for j in range(8)]
    inside = (lane >= at) & (lane < at + 8)
    r = jnp.where(inside, (lane - at == sub).astype(F32), w[b])
    t = r
    pivots = jnp.ones((8, H), F32)
    inverses = []
    for k in range(0, 8, 2):
        first, second = sub == k, sub == k + 1
        p, q, o = row_of(c[k], k), row_of(c[k + 1], k), row_of(c[k + 1], k + 1)
        det = 1.0 / (p * o - q * q)
        m0 = jnp.where(first | second, 0.0, c[k])
        m1 = jnp.where(first | second, 0.0, c[k + 1])
        f0 = (m0 * o - m1 * q) * det
        f1 = (m1 * p - m0 * q) * det
        inverses.append((o * det, -q * det, p * det))
        ratio = q * (1.0 / p)
        r0, r1 = row_of(r, k), row_of(r, k + 1)
        t = jnp.where(first, r0, jnp.where(second, r1 - ratio * r0, t))
        pivots = jnp.where(first, p, jnp.where(second, o - ratio * q, pivots))
        for j in range(k + 2, 8):
            c[j] = c[j] - (f0 * row_of(c[j], k) + f1 * row_of(c[j], k + 1))
        r = r - (f0 * r0 + f1 * r1)
    if b < 15:
        rows = []
        for k in range(0, 8, 2):
            ia, ib, ic = inverses[k // 2]
            r0, r1 = row_of(r, k), row_of(r, k + 1)
            rows += [ia * r0 + ib * r1, ib * r0 + ic * r1]
        for i in range(b + 1, 16):
            cols = [lane_of(w[i], at + j) for j in range(8)]
            w[i] = jnp.where(inside, 0.0, w[i]) - sum8([cols[j] * rows[j] for j in range(8)])
    return jnp.where(lane < at + 8, t * lax.rsqrt(pivots), 0.0)


def factor_part(w, blocks):
    sub = lax.broadcasted_iota(jnp.int32, (8, H), 0)
    lane = lax.broadcasted_iota(jnp.int32, (8, H), 1)
    return [pivot_block(w, b, sub, lane) for b in blocks]


def groups(a):
    return [a[8 * r : 8 * r + 8, :] for r in range(16)]


def factor_start(block, f1):
    f1[...] = jnp.concatenate(factor_part(groups(block[0:H, 0:H]), range(16)), axis=0)


def factor_rest(block, fill, x, v, f1, f2, z):
    z[...] = nt(block[H:N, 0:H], f1[...])
    w = groups(block[H:N, H:N] - nt(z[...], z[...]))
    out = factor_part(w, range(8))
    fill()
    v[:, 0:H] = nt(x[:, 0:H], f1[...])
    y = x[:, H:N] - nt(v[:, 0:H], z[...])
    out += factor_part(w, range(8, 16))
    f2[...] = jnp.concatenate(out, axis=0)
    v[:, H:N] = nt(y, f2[...])


def means(v, f1, f2, z):
    hi = nn(v[:, H:N], f2[...])
    lo = nn(v[:, 0:H] - nn(hi, z[...]), f1[...])
    return lo, hi


def kernel(
    diag, coup, info, out,
    d1, c0, c1, hin, d2, xl, xu, xcat, v1, v2, f1a, f2a, za, f1b, f2b, zb, ga, gb,
    own_h, rc1, rc2, rxl, rxu, pu01, pu02, sx0, pl1, pl2, pu1, pu2, sx, xin, xown,
    g1_send, g1_recv, g2_send, g2_recv, r1_recv, r2_recv, rx_recv, s_send, x_send, x_recv, own_sem,
):
    s = lax.axis_index("tm")
    j = lax.axis_index("state")
    rows = pl.ds(pl.multiple_of(j * 32, 32), 32)

    def divides(d):
        return lax.rem(s, d) == 0

    even = divides(2)

    barrier = pltpu.get_barrier_semaphore()
    count = jnp.int32(7)
    for r in range(1, 8):
        pl.semaphore_signal(
            barrier, inc=1, device_id=(s, lax.rem(j + r, 8)), device_id_type=MESH
        )
    for k in range(6):
        d = 2**k
        down = divides(d) & (s >= d)
        up = divides(d) & (s + d < 64)
        count = count + down.astype(jnp.int32) + up.astype(jnp.int32)

        @pl.when(down)
        def _():
            pl.semaphore_signal(barrier, inc=1, device_id=(s - d, j), device_id_type=MESH)

        @pl.when(up)
        def _():
            pl.semaphore_signal(barrier, inc=1, device_id=(s + d, j), device_id_type=MESH)

    first = [
        (diag.at[1], d1.at[rows]),
        (coup.at[0], c0.at[rows]),
        (coup.at[1], c1.at[rows]),
        (info, hin.at[pl.ds(pl.multiple_of(j * 8, 8), 8)]),
        (diag.at[0], d2.at[rows]),
    ]
    local = [
        pltpu.make_async_copy(src, dst, own_sem.at[a]) for a, (src, dst) in enumerate(first)
    ]
    for c in local:
        c.start()

    pl.semaphore_wait(barrier, count)

    def to(src, dst, send, recv, tm, state):
        return pltpu.make_async_remote_copy(
            src_ref=src, dst_ref=dst, send_sem=send, recv_sem=recv,
            device_id=(tm, state), device_id_type=MESH,
        )

    def peer(src, dst, sends, recvs, a, r):
        return to(src, dst, sends.at[a, r], recvs.at[a, r], s, lax.rem(j + r, 8))

    for a, (src, dst) in enumerate(first):
        for r in range(1, 8):
            peer(src, dst, g1_send, g1_recv, a, r).start()

    def arrived(a):
        src, dst = first[a]
        local[a].wait()
        for r in range(1, 8):
            peer(src, dst, g1_send, g1_recv, a, r).wait_recv()

    arrived(0)
    factor_start(d1, f1a)

    def fill0():
        arrived(1)
        arrived(2)
        arrived(3)
        info_all = sum8([hin[8 * i : 8 * i + 8, :] for i in range(8)])
        own_h[...] = row_of(info_all, 0)
        xcat[0:N, :] = c0[...]
        xcat[N : 2 * N, :] = jnp.where(s == 63, 0.0, c1[...].T)
        xcat[2 * N : 2 * N + 8, :] = row_of(info_all, 1)

    factor_rest(d1, fill0, xcat, v1, f1a, f2a, za)

    start = pl.multiple_of(j * 32, 32)
    up0 = s < 63

    def up0_sends(act):
        @pl.when(up0)
        def _():
            act(to(pu01, rc1.at[0], s_send.at[0], r1_recv.at[0], s + 1, j))

    def up0_rest(act):
        @pl.when(up0)
        def _():
            act(to(pu02, rc2.at[0], s_send.at[1], r2_recv.at[0], s + 1, j))

    def up0_link(act):
        @pl.when(even)
        def _():
            act(to(sx0, rxl, s_send.at[2], rx_recv.at[0], s + 1, j))

    pu01[...] = nt(v1[N : N + H, :], v1[N : N + H, :])
    up0_sends(lambda c: c.start())
    sx0[...] = -nt(v1[pl.ds(start, 32), :], v1[N : 2 * N, :])
    up0_link(lambda c: c.start())
    pu02[0:H, :] = nt(v1[N + H : 2 * N, :], v1[N : 2 * N, :])
    back = nt(v1[2 * N : 2 * N + 8, :], v1[0 : 2 * N, :])
    pu02[H : H + 8, :] = back[:, N : 2 * N]
    up0_rest(lambda c: c.start())
    own_h[...] = own_h[...] - back[:, 0:N]
    arrived(4)
    d2[...] = d2[...] - nt(v1[0:N, :], v1[0:N, :])

    @pl.when(jnp.logical_not(even))
    def _():
        xu[...] = -nt(v1[N : 2 * N, :], v1[0:N, :])

    def take_lead(slot):
        to(pl1, rc1.at[slot], s_send.at[3], r1_recv.at[slot], s, j).wait_recv()
        d2[0:H, 0:H] = d2[0:H, 0:H] - rc1[slot]

    def take_rest(slot):
        to(pl2, rc2.at[slot], s_send.at[4], r2_recv.at[slot], s, j).wait_recv()
        d2[H:N, :] = d2[H:N, :] - rc2[slot, 0:H, :]
        own_h[...] = own_h[...] - rc2[slot, H : H + 8, :]

    @pl.when(even & (s > 0))
    def _():
        take_lead(0)
        take_rest(0)

    last = [jnp.logical_not(even)]
    for k in range(6):
        at_last = lax.rem(s, 4 * 2**k) == 2 * 2**k
        if k == 5:
            at_last = s == 0
        last.append(at_last)
        early = divides(4 * 2**k) & jnp.logical_not(at_last)

        @pl.when(early & (s > 0))
        def _():
            take_lead(1 + 2 * k)
            take_rest(1 + 2 * k)

        @pl.when(early)
        def _():
            take_lead(2 + 2 * k)
            take_rest(2 + 2 * k)

    def take_last(take):
        @pl.when(last[0])
        def _():
            take(0)

        for k in range(6):
            if k < 5:

                @pl.when(last[k + 1])
                def _():
                    take(1 + 2 * k)

            @pl.when(last[k + 1])
            def _():
                take(2 + 2 * k)

    take_last(take_lead)
    factor_start(d2, f1b)
    take_last(take_rest)

    def each_peer(src, dst, a, act):
        for r in range(1, 8):
            act(peer(src, dst, g2_send, g2_recv, a, r))

    @pl.when(s > 0)
    def _():
        to(sx0, rxl, s_send.at[2], rx_recv.at[0], s, j).wait_recv()
        each_peer(rxl, xl.at[rows], 0, lambda c: c.start())
        xl[rows, :] = rxl[...]

        @pl.when(even)
        def _():
            to(sx, rxu, s_send.at[7], rx_recv.at[1], s, j).wait_recv()
            each_peer(rxu, xu.at[rows], 1, lambda c: c.start())
            xu[rows, :] = rxu[...]

    def fill():
        @pl.when(s > 0)
        def _():
            each_peer(rxl, xl.at[rows], 0, lambda c: c.wait_recv())

            @pl.when(even)
            def _():
                each_peer(rxu, xu.at[rows], 1, lambda c: c.wait_recv())

            xcat[0:N, :] = xl[...]
            xcat[N : 2 * N, :] = xu[...]

        @pl.when(s == 0)
        def _():
            xcat[0 : 2 * N, :] = jnp.zeros((2 * N, N), F32)

        xcat[2 * N : 2 * N + 8, :] = own_h[...]

    factor_rest(d2, fill, xcat, v2, f1b, f2b, zb)

    own_level = []
    to_lower = jnp.bool_(False)
    for k in range(6):
        d = 2**k
        mine = lax.rem(s, 2 * d) == d
        own_level.append((k, d, mine))
        to_lower = to_lower | (mine & (lax.rem(s - d, 4 * d) == 2 * d))

    def sends(lower, upper, lower_dst, upper_dst, recv, at, act):
        for k, d, mine in own_level:

            @pl.when(mine)
            def _():
                slot = 2 + 2 * k
                act(to(lower, lower_dst.at[slot], s_send.at[at], recv.at[slot], s - d, j))

            @pl.when(mine & (s + d < 64))
            def _():
                slot = 1 + 2 * k
                act(to(upper, upper_dst.at[slot], s_send.at[at + 1], recv.at[slot], s + d, j))

    def lead_sends(act):
        sends(pl1, pu1, rc1, rc1, r1_recv, 3, act)

    def rest_sends(act):
        sends(pl2, pu2, rc2, rc2, r2_recv, 5, act)

    def link_sends(act):
        for k, d, mine in own_level[:5]:

            @pl.when(mine & (lax.rem(s - d, 4 * d) == 2 * d))
            def _():
                act(to(sx, rxu, s_send.at[7], rx_recv.at[1], s - d, j))

            @pl.when(mine & (s + d < 64) & (lax.rem(s + d, 4 * d) == 2 * d))
            def _():
                act(to(sx, rxl, s_send.at[7], rx_recv.at[0], s + d, j))

    @pl.when(s > 0)
    def _():
        pl1[...] = nt(v2[0:H, :], v2[0:H, :])
        pu1[...] = nt(v2[N : N + H, :], v2[N : N + H, :])

    lead_sends(lambda c: c.start())

    @pl.when(to_lower)
    def _():
        sx[...] = -nt(v2[pl.ds(start + N, 32), :], v2[0:N, :])

    @pl.when(jnp.logical_not(to_lower) & (s > 0))
    def _():
        sx[...] = -nt(v2[pl.ds(start, 32), :], v2[N : 2 * N, :])

    link_sends(lambda c: c.start())

    @pl.when(s > 0)
    def _():
        pl2[0:H, :] = nt(v2[H:N, :], v2[0:N, :])
        pu2[0:H, :] = nt(v2[N + H : 2 * N, :], v2[N : 2 * N, :])
        back = nt(v2[2 * N : 2 * N + 8, :], v2[0 : 2 * N, :])
        pl2[H : H + 8, :] = back[:, 0:N]
        pu2[H : H + 8, :] = back[:, N : 2 * N]

    rest_sends(lambda c: c.start())

    @pl.when(s > 0)
    def _():
        lo, hi = means(v2, f1b, f2b, zb)
        gb[:, 0:H] = lo
        gb[:, H:N] = hi

    for k, d, mine in own_level:

        @pl.when(mine)
        def _():
            to(xown, xin.at[0], x_send.at[0], x_recv.at[0], s, j).wait_recv()

        @pl.when(mine & (s + d < 64))
        def _():
            to(xown, xin.at[1], x_send.at[0], x_recv.at[1], s, j).wait_recv()

        @pl.when(mine & (s + d >= 64))
        def _():
            xin[1] = jnp.zeros((8, N), F32)

    @pl.when(s == 0)
    def _():
        lo, hi = means(v2[2 * N : 2 * N + 8, :], f1b, f2b, zb)
        xown[:, 0:H] = lo
        xown[:, H:N] = hi

    @pl.when(s > 0)
    def _():
        xown[...] = gb[2 * N : 2 * N + 8, :] - (
            nn(xin[0], gb[0:N, :]) + nn(xin[1], gb[N : 2 * N, :])
        )

    def spread(act):
        for k in reversed(range(6)):
            d = 2**k

            @pl.when(divides(2 * d))
            def _():
                act(to(xown, xin.at[0], x_send.at[2 * k], x_recv.at[0], s + d, j))

            @pl.when(divides(2 * d) & (s > 0))
            def _():
                act(to(xown, xin.at[1], x_send.at[2 * k + 1], x_recv.at[1], s - d, j))

        @pl.when(jnp.logical_not(even))
        def _():
            act(to(xown, xin.at[2], x_send.at[12], x_recv.at[2], s - 1, j))

    spread(lambda c: c.start())

    lo, hi = means(v1, f1a, f2a, za)
    ga[:, 0:H] = lo
    ga[:, H:N] = hi
    part = ga[2 * N : 2 * N + 8, :] - nn(xown[...], ga[0:N, :])

    @pl.when(even)
    def _():
        to(xown, xin.at[2], x_send.at[12], x_recv.at[2], s, j).wait_recv()

    @pl.when(jnp.logical_not(even))
    def _():
        xin[2] = xin[1]

    later = part - nn(xin[2], ga[N : 2 * N, :])
    both = jnp.concatenate([xown[0:1, :], later[0:1, :]], axis=0)
    for i in range(8):

        @pl.when(j == i)
        def _():
            out[...] = both[:, 32 * i : 32 * i + 32]

    for a, (src, dst) in enumerate(first):
        for r in range(1, 8):
            peer(src, dst, g1_send, g1_recv, a, r).wait_send()

    up0_sends(lambda c: c.wait_send())
    up0_link(lambda c: c.wait_send())
    up0_rest(lambda c: c.wait_send())

    @pl.when(s > 0)
    def _():
        each_peer(rxl, xl.at[rows], 0, lambda c: c.wait_send())

        @pl.when(even)
        def _():
            each_peer(rxu, xu.at[rows], 1, lambda c: c.wait_send())

    lead_sends(lambda c: c.wait_send())
    link_sends(lambda c: c.wait_send())
    rest_sends(lambda c: c.wait_send())
    spread(lambda c: c.wait_send())


def body(diagonal, coupling, info):
    offset = lax.axis_index("state") * 32
    placed = lax.dynamic_update_slice(jnp.zeros((8, N), F32), info, (0, offset))
    vmem = pltpu.VMEM
    dma = pltpu.SemaphoreType.DMA
    square = vmem((N, N), F32)
    half = vmem((H, H), F32)
    tall = vmem((2 * N + 8, N), F32)
    slab = vmem((H + 8, N), F32)
    slice_ = vmem((32, N), F32)
    return pl.pallas_call(
        kernel,
        out_shape=jax.ShapeDtypeStruct((2, 32), F32),
        in_specs=[pl.BlockSpec(memory_space=pl.ANY)] * 3,
        out_specs=pl.BlockSpec(memory_space=vmem),
        scratch_shapes=[
            square, square, square, vmem((64, N), F32), square, square, square, tall, tall, tall,
            half, half, half, half, half, half, tall, tall,
            vmem((8, N), F32), vmem((13, H, H), F32), vmem((13, H + 8, N), F32),
            slice_, slice_, half, slab, slice_, half, slab, half, slab, slice_,
            vmem((3, 8, N), F32), vmem((8, N), F32),
            dma((5, 8)), dma((5, 8)), dma((2, 8)), dma((2, 8)),
            dma((13,)), dma((13,)), dma((2,)), dma((8,)), dma((13,)), dma((3,)), dma((5,)),
        ],
        compiler_params=pltpu.CompilerParams(
            collective_id=0, has_side_effects=True, vmem_limit_bytes=32 * 1024 * 1024
        ),
    )(diagonal, coupling, placed)


def solution(mesh):
    placed = (P("tm", "state", None), P("tm", "state", None), P("tm", "state"))
    return jax.shard_map(
        body, mesh=mesh, in_specs=placed, out_specs=P("tm", "state"), check_vma=False
    )
```

time: 252 us -> 187 us (0.74)
  Pallas kernels: 248 us -> 183 us
    pallas_call x1, Pallas kernels: 248 us -> 183 us  [body(): pl.pallas_call(kernel, out_shape=jax.ShapeDtypeStruct((2, 32), F32), in_s...]
where the time goes in v2:
time: 187 us; the launch traced here: 186 us
  Pallas kernels  183 us (98%)
  local copies, waits for them, and re-layouts  3.15 us (2%)
    pallas_call x1, Pallas kernels, body(): pl.pallas_call(kernel, out_shape=jax.ShapeDtypeStruct((2, 32), F32), in_s...  183 us

profile of v2, /device:TPU:8, one launch (start us, length us, event | category | flops | bytes accessed | tf_op | source)
XLA Modules:
  0.0 186.3 jit_solution(8195365959181051015)
XLA Ops:
  0.0 0.0 copy-start.2
  0.0 0.7 copy-done.2
  0.7 0.2 dynamic_update_slice.3.info
  0.9 0.0 copy-start
  0.9 0.8 copy-done
  1.8 0.0 copy-start.1
  1.8 0.8 copy-done.1
  2.6 183.2 %shard_map.37 = f32[2,32]{1,0:T(2,128)S(1)} custom-call(f32[2,32,256]{2,1,0:T(8,128)S(1)} %copy-done, f32[2,32,256]{2,1,0:T(8,128)S(1)} %copy-done.1, f32[8,256]{1,0:T(8,128)S(1)} %dynamic_update_slice.3.info), custom_call_target="tpu_custom_call" | custom-call | tf_op jit(solution)/shard_map/pallas_call | solution.py:479
  185.8 0.6 copy.6
  (1 shorter events, 0.0 us)
Async XLA Ops:
  0.0 0.7 copy-start.2
  0.9 0.8 copy-start
  1.8 0.8 copy-start.1

commit v3 on v2

--- a/solution.py
+++ b/solution.py
@@ -80,20 +80,36 @@
     return [a[8 * r : 8 * r + 8, :] for r in range(16)]
 
 
-def factor_start(block, f1):
-    f1[...] = jnp.concatenate(factor_part(groups(block[0:H, 0:H]), range(16)), axis=0)
-
-
-def factor_rest(block, fill, x, v, f1, f2, z):
+def factor_start(block, begin, f1):
+    w = groups(block[0:H, 0:H])
+    out = factor_part(w, range(4))
+    begin()
+    out += factor_part(w, range(4, 16))
+    f1[...] = jnp.concatenate(out, axis=0)
+
+
+def factor_rest(block, fill, x, v, y, f1, f2, z, lead):
     z[...] = nt(block[H:N, 0:H], f1[...])
     w = groups(block[H:N, H:N] - nt(z[...], z[...]))
-    out = factor_part(w, range(8))
+    out = factor_part(w, range(12))
     fill()
     v[:, 0:H] = nt(x[:, 0:H], f1[...])
-    y = x[:, H:N] - nt(v[:, 0:H], z[...])
-    out += factor_part(w, range(8, 16))
+    y[...] = x[:, H:N] - nt(v[:, 0:H], z[...])
+    for at, to in lead:
+        to[...] = nt(v[at : at + H, 0:H], v[at : at + H, 0:H])
+    out += factor_part(w, range(12, 16))
     f2[...] = jnp.concatenate(out, axis=0)
-    v[:, H:N] = nt(y, f2[...])
+    for at, to in lead:
+        top = nt(y[at : at + H, :], f2[...])
+        v[at : at + H, H:N] = top
+        to[...] = to[...] + nt(top, top)
+
+
+def finish_rows(v, y, f2, done):
+    at = [r for r in (0, H, N, N + H) if r not in done]
+    for r in at:
+        v[r : r + H, H:N] = nt(y[r : r + H, :], f2[...])
+    v[2 * N : 2 * N + 8, H:N] = nt(y[2 * N : 2 * N + 8, :], f2[...])
 
 
 def means(v, f1, f2, z):
@@ -104,7 +120,7 @@
 
 def kernel(
     diag, coup, info, out,
-    d1, c0, c1, hin, d2, xl, xu, xcat, v1, v2, f1a, f2a, za, f1b, f2b, zb, ga, gb,
+    d1, c0, c1, hin, d2, xl, xu, xcat, ycat, v1, v2, f1a, f2a, za, f1b, f2b, zb, ga, gb,
     own_h, rc1, rc2, rxl, rxu, pu01, pu02, sx0, pl1, pl2, pu1, pu2, sx, xin, xown,
     g1_send, g1_recv, g2_send, g2_recv, r1_recv, r2_recv, rx_recv, s_send, x_send, x_recv, own_sem,
 ):
@@ -161,18 +177,22 @@
     def peer(src, dst, sends, recvs, a, r):
         return to(src, dst, sends.at[a, r], recvs.at[a, r], s, lax.rem(j + r, 8))
 
-    for a, (src, dst) in enumerate(first):
+    def gather(a, act):
+        src, dst = first[a]
         for r in range(1, 8):
-            peer(src, dst, g1_send, g1_recv, a, r).start()
+            act(peer(src, dst, g1_send, g1_recv, a, r))
+
+    gather(0, lambda c: c.start())
+    gather(0, lambda c: c.wait_send())
+    for a in range(1, 5):
+        gather(a, lambda c: c.start())
 
     def arrived(a):
-        src, dst = first[a]
         local[a].wait()
-        for r in range(1, 8):
-            peer(src, dst, g1_send, g1_recv, a, r).wait_recv()
+        gather(a, lambda c: c.wait_recv())
 
     arrived(0)
-    factor_start(d1, f1a)
+    factor_start(d1, lambda: None, f1a)
 
     def fill0():
         arrived(1)
@@ -184,7 +204,7 @@
         xcat[N : 2 * N, :] = jnp.where(s == 63, 0.0, c1[...].T)
         xcat[2 * N : 2 * N + 8, :] = row_of(info_all, 1)
 
-    factor_rest(d1, fill0, xcat, v1, f1a, f2a, za)
+    factor_rest(d1, fill0, xcat, v1, ycat, f1a, f2a, za, [(N, pu01)])
 
     start = pl.multiple_of(j * 32, 32)
     up0 = s < 63
@@ -204,8 +224,8 @@
         def _():
             act(to(sx0, rxl, s_send.at[2], rx_recv.at[0], s + 1, j))
 
-    pu01[...] = nt(v1[N : N + H, :], v1[N : N + H, :])
     up0_sends(lambda c: c.start())
+    finish_rows(v1, ycat, f2a, [N])
     sx0[...] = -nt(v1[pl.ds(start, 32), :], v1[N : 2 * N, :])
     up0_link(lambda c: c.start())
     pu02[0:H, :] = nt(v1[N + H : 2 * N, :], v1[N : 2 * N, :])
@@ -269,24 +289,23 @@
                 take(2 + 2 * k)
 
     take_last(take_lead)
-    factor_start(d2, f1b)
-    take_last(take_rest)
 
     def each_peer(src, dst, a, act):
         for r in range(1, 8):
             act(peer(src, dst, g2_send, g2_recv, a, r))
 
-    @pl.when(s > 0)
-    def _():
-        to(sx0, rxl, s_send.at[2], rx_recv.at[0], s, j).wait_recv()
-        each_peer(rxl, xl.at[rows], 0, lambda c: c.start())
-        xl[rows, :] = rxl[...]
-
-        @pl.when(even)
-        def _():
-            to(sx, rxu, s_send.at[7], rx_recv.at[1], s, j).wait_recv()
-            each_peer(rxu, xu.at[rows], 1, lambda c: c.start())
-            xu[rows, :] = rxu[...]
+    def begin():
+        @pl.when(s > 0)
+        def _():
+            to(sx0, rxl, s_send.at[2], rx_recv.at[0], s, j).wait_recv()
+            each_peer(rxl, xl.at[rows], 0, lambda c: c.start())
+            xl[rows, :] = rxl[...]
+
+            @pl.when(even)
+            def _():
+                to(sx, rxu, s_send.at[7], rx_recv.at[1], s, j).wait_recv()
+                each_peer(rxu, xu.at[rows], 1, lambda c: c.start())
+                xu[rows, :] = rxu[...]
 
     def fill():
         @pl.when(s > 0)
@@ -306,7 +325,9 @@
 
         xcat[2 * N : 2 * N + 8, :] = own_h[...]
 
-    factor_rest(d2, fill, xcat, v2, f1b, f2b, zb)
+    factor_start(d2, begin, f1b)
+    take_last(take_rest)
+    factor_rest(d2, fill, xcat, v2, ycat, f1b, f2b, zb, [(0, pl1), (N, pu1)])
 
     own_level = []
     to_lower = jnp.bool_(False)
@@ -346,12 +367,8 @@
             def _():
                 act(to(sx, rxl, s_send.at[7], rx_recv.at[0], s + d, j))
 
-    @pl.when(s > 0)
-    def _():
-        pl1[...] = nt(v2[0:H, :], v2[0:H, :])
-        pu1[...] = nt(v2[N : N + H, :], v2[N : N + H, :])
-
     lead_sends(lambda c: c.start())
+    finish_rows(v2, ycat, f2b, [0, N])
 
     @pl.when(to_lower)
     def _():
@@ -379,6 +396,15 @@
         gb[:, 0:H] = lo
         gb[:, H:N] = hi
 
+    def early_means():
+        lo, hi = means(v1, f1a, f2a, za)
+        ga[:, 0:H] = lo
+        ga[:, H:N] = hi
+
+    @pl.when(s > 0)
+    def _():
+        early_means()
+
     for k, d, mine in own_level:
 
         @pl.when(mine)
@@ -423,9 +449,10 @@
 
     spread(lambda c: c.start())
 
-    lo, hi = means(v1, f1a, f2a, za)
-    ga[:, 0:H] = lo
-    ga[:, H:N] = hi
+    @pl.when(s == 0)
+    def _():
+        early_means()
+
     part = ga[2 * N : 2 * N + 8, :] - nn(xown[...], ga[0:N, :])
 
     @pl.when(even)
@@ -444,9 +471,8 @@
         def _():
             out[...] = both[:, 32 * i : 32 * i + 32]
 
-    for a, (src, dst) in enumerate(first):
-        for r in range(1, 8):
-            peer(src, dst, g1_send, g1_recv, a, r).wait_send()
+    for a in range(1, 5):
+        gather(a, lambda c: c.wait_send())
 
     up0_sends(lambda c: c.wait_send())
     up0_link(lambda c: c.wait_send())
@@ -479,10 +505,10 @@
     return pl.pallas_call(
         kernel,
         out_shape=jax.ShapeDtypeStruct((2, 32), F32),
-        in_specs=[pl.BlockSpec(memory_space=pl.ANY)] * 3,
+        in_specs=[pl.BlockSpec(memory_space=pltpu.HBM)] * 3,
         out_specs=pl.BlockSpec(memory_space=vmem),
         scratch_shapes=[
-            square, square, square, vmem((64, N), F32), square, square, square, tall, tall, tall,
+            square, square, square, vmem((64, N), F32), square, square, square, tall, vmem((2 * N + 8, H), F32), tall, tall,
             half, half, half, half, half, half, tall, tall,
             vmem((8, N), F32), vmem((13, H, H), F32), vmem((13, H + 8, N), F32),
             slice_, slice_, half, slab, slice_, half, slab, half, slab, slice_,

time: 187 us -> 166 us (0.89)
  the two profiles are of different devices: /device:TPU:8 before, /device:TPU:16 now
where the time goes in v3:
time: 166 us
  Pallas kernels  163 us (98%)
  local copies, waits for them, and re-layouts  3.15 us (2%)
    pallas_call x1, Pallas kernels, body(): pl.pallas_call(kernel, out_shape=jax.ShapeDtypeStruct((2, 32), F32), in_s...  163 us

profile of v3, /device:TPU:16, one launch (start us, length us, event | category | flops | bytes accessed | tf_op | source)
XLA Modules:
  0.0 165.8 jit_solution(12029112502485160752)
XLA Ops:
  0.0 0.0 copy-start.2
  0.0 0.7 copy-done.2
  0.7 0.2 dynamic_update_slice.3.info
  0.9 0.0 copy-start
  0.9 0.8 copy-done
  1.8 0.0 copy-start.1
  1.8 0.8 copy-done.1
  2.6 162.7 %shard_map.37 = f32[2,32]{1,0:T(2,128)S(1)} custom-call(f32[2,32,256]{2,1,0:T(8,128)S(1)} %copy-done, f32[2,32,256]{2,1,0:T(8,128)S(1)} %copy-done.1, f32[8,256]{1,0:T(8,128)S(1)} %dynamic_update_slice.3.info), custom_call_target="tpu_custom_call" | custom-call | tf_op jit(solution)/shard_map/pallas_call | solution.py:505
  165.3 0.6 copy.6
  (1 shorter events, 0.0 us)
Async XLA Ops:
  0.0 0.7 copy-start.2
  0.9 0.8 copy-start
  1.8 0.8 copy-start.1

commit v4 on v3

--- a/solution.py
+++ b/solution.py
@@ -7,6 +7,7 @@
 
 N = 256
 H = 128
+Q = 64
 F32 = jnp.float32
 MESH = pl.DeviceIdType.MESH
 EXACT = lax.Precision.HIGHEST
@@ -82,16 +83,18 @@
 
 def factor_start(block, begin, f1):
     w = groups(block[0:H, 0:H])
-    out = factor_part(w, range(4))
+    out = factor_part(w, range(8))
     begin()
-    out += factor_part(w, range(4, 16))
+    out += factor_part(w, range(8, 16))
     f1[...] = jnp.concatenate(out, axis=0)
 
 
-def factor_rest(block, fill, x, v, y, f1, f2, z, lead):
+def factor_rest(block, pass_on, fill, x, v, y, f1, f2, z, lead):
     z[...] = nt(block[H:N, 0:H], f1[...])
     w = groups(block[H:N, H:N] - nt(z[...], z[...]))
-    out = factor_part(w, range(12))
+    out = factor_part(w, range(2))
+    pass_on()
+    out += factor_part(w, range(2, 12))
     fill()
     v[:, 0:H] = nt(x[:, 0:H], f1[...])
     y[...] = x[:, H:N] - nt(v[:, 0:H], z[...])
@@ -121,12 +124,17 @@
 def kernel(
     diag, coup, info, out,
     d1, c0, c1, hin, d2, xl, xu, xcat, ycat, v1, v2, f1a, f2a, za, f1b, f2b, zb, ga, gb,
-    own_h, rc1, rc2, rxl, rxu, pu01, pu02, sx0, pl1, pl2, pu1, pu2, sx, xin, xown,
-    g1_send, g1_recv, g2_send, g2_recv, r1_recv, r2_recv, rx_recv, s_send, x_send, x_recv, own_sem,
+    own_h, rc1, rc2, dsib, pu01, pu02, sx0, pl1, pl2, pu1, pu2, sx, xin, xown,
+    g1_send, g1_recv, sib_send, sib_recv, r1_recv, r2_recv, rx_recv, s_send, x_send, x_recv, own_sem,
 ):
     s = lax.axis_index("tm")
     j = lax.axis_index("state")
+    core = lax.rem(j, 2)
+    sibling = j + 1 - 2 * core
     rows = pl.ds(pl.multiple_of(j * 32, 32), 32)
+    half_rows = pl.ds(pl.multiple_of(core * H, H), H)
+    own_rows = pl.ds(pl.multiple_of(H + core * Q, Q), Q)
+    other_rows = pl.ds(pl.multiple_of(H + Q - core * Q, Q), Q)
 
     def divides(d):
         return lax.rem(s, d) == 0
@@ -182,31 +190,62 @@
         for r in range(1, 8):
             act(peer(src, dst, g1_send, g1_recv, a, r))
 
+    def direct(a, act):
+        src, dst = first[a]
+        for r in (2, 4, 6):
+            act(peer(src, dst, g1_send, g1_recv, a, r))
+        act(to(src, dst, g1_send.at[a, 1], g1_recv.at[a, 1], s, sibling))
+
+    def hand_on(a, act):
+        whole = (None, c0, c1, None, d2)[a]
+        for r in (2, 4, 6):
+            at = pl.ds(pl.multiple_of(lax.rem(j + 8 - r, 8) * 32, 32), 32)
+            piece = whole.at[at]
+            act(to(piece, piece, g1_send.at[a, r + 1], g1_recv.at[a, r + 1], s, sibling))
+
+    def direct_arrived(a):
+        src, dst = first[a]
+        for r in (2, 4, 6):
+            peer(src, dst, g1_send, g1_recv, a, r).wait_recv()
+
+    def arrived(a):
+        src, dst = first[a]
+        local[a].wait()
+        to(src, dst, g1_send.at[a, 1], g1_recv.at[a, 1], s, sibling).wait_recv()
+        hand_on(a, lambda c: c.wait_recv())
+
     gather(0, lambda c: c.start())
     gather(0, lambda c: c.wait_send())
-    for a in range(1, 5):
-        gather(a, lambda c: c.start())
-
-    def arrived(a):
-        local[a].wait()
-        gather(a, lambda c: c.wait_recv())
-
-    arrived(0)
+    for a in (1, 2, 4):
+        direct(a, lambda c: c.start())
+    gather(3, lambda c: c.start())
+
+    local[0].wait()
+    gather(0, lambda c: c.wait_recv())
     factor_start(d1, lambda: None, f1a)
 
+    def pass_on0():
+        for a in (1, 2):
+            direct_arrived(a)
+            hand_on(a, lambda c: c.start())
+
     def fill0():
+        direct_arrived(4)
+        hand_on(4, lambda c: c.start())
         arrived(1)
         arrived(2)
-        arrived(3)
+        local[3].wait()
+        gather(3, lambda c: c.wait_recv())
         info_all = sum8([hin[8 * i : 8 * i + 8, :] for i in range(8)])
         own_h[...] = row_of(info_all, 0)
         xcat[0:N, :] = c0[...]
         xcat[N : 2 * N, :] = jnp.where(s == 63, 0.0, c1[...].T)
         xcat[2 * N : 2 * N + 8, :] = row_of(info_all, 1)
 
-    factor_rest(d1, fill0, xcat, v1, ycat, f1a, f2a, za, [(N, pu01)])
-
-    start = pl.multiple_of(j * 32, 32)
+    factor_rest(d1, pass_on0, fill0, xcat, v1, ycat, f1a, f2a, za, [(N, pu01)])
+
+    half_at = pl.multiple_of(core * H, H)
+    own_at = pl.multiple_of(H + core * Q, Q)
     up0 = s < 63
 
     def up0_sends(act):
@@ -222,19 +261,21 @@
     def up0_link(act):
         @pl.when(even)
         def _():
-            act(to(sx0, rxl, s_send.at[2], rx_recv.at[0], s + 1, j))
+            act(to(sx0, xl.at[half_rows], s_send.at[2], rx_recv.at[0], s + 1, j))
 
     up0_sends(lambda c: c.start())
     finish_rows(v1, ycat, f2a, [N])
-    sx0[...] = -nt(v1[pl.ds(start, 32), :], v1[N : 2 * N, :])
+    pu02[0:Q, :] = nt(v1[pl.ds(own_at + N, Q), :], v1[N : 2 * N, :])
+    back = nt(v1[2 * N : 2 * N + 8, :], v1[0 : 2 * N, :])
+    pu02[Q : Q + 8, :] = back[:, N : 2 * N]
+    up0_rest(lambda c: c.start())
+    sx0[...] = -nt(v1[pl.ds(half_at, H), :], v1[N : 2 * N, :])
     up0_link(lambda c: c.start())
-    pu02[0:H, :] = nt(v1[N + H : 2 * N, :], v1[N : 2 * N, :])
-    back = nt(v1[2 * N : 2 * N + 8, :], v1[0 : 2 * N, :])
-    pu02[H : H + 8, :] = back[:, N : 2 * N]
-    up0_rest(lambda c: c.start())
     own_h[...] = own_h[...] - back[:, 0:N]
     arrived(4)
-    d2[...] = d2[...] - nt(v1[0:N, :], v1[0:N, :])
+    hand_on(4, lambda c: c.wait_send())
+    d2[0:H, 0:H] = d2[0:H, 0:H] - nt(v1[0:H, :], v1[0:H, :])
+    d2[own_rows, :] = d2[own_rows, :] - nt(v1[own_rows, :], v1[0:N, :])
 
     @pl.when(jnp.logical_not(even))
     def _():
@@ -246,8 +287,8 @@
 
     def take_rest(slot):
         to(pl2, rc2.at[slot], s_send.at[4], r2_recv.at[slot], s, j).wait_recv()
-        d2[H:N, :] = d2[H:N, :] - rc2[slot, 0:H, :]
-        own_h[...] = own_h[...] - rc2[slot, H : H + 8, :]
+        d2[own_rows, :] = d2[own_rows, :] - rc2[slot, 0:Q, :]
+        own_h[...] = own_h[...] - rc2[slot, Q : Q + 8, :]
 
     @pl.when(even & (s > 0))
     def _():
@@ -290,31 +331,41 @@
 
     take_last(take_lead)
 
-    def each_peer(src, dst, a, act):
-        for r in range(1, 8):
-            act(peer(src, dst, g2_send, g2_recv, a, r))
+    def hand(ref_rows, dst, a):
+        return to(ref_rows, dst, sib_send.at[a], sib_recv.at[a], s, sibling)
+
+    def hand_rest():
+        return hand(d2.at[own_rows], dsib, 0)
+
+    def hand_xl():
+        return hand(xl.at[half_rows], xl.at[half_rows], 1)
+
+    def hand_xu():
+        return hand(xu.at[half_rows], xu.at[half_rows], 2)
 
     def begin():
+        take_last(take_rest)
+        hand_rest().start()
+
+    def pass_on():
         @pl.when(s > 0)
         def _():
-            to(sx0, rxl, s_send.at[2], rx_recv.at[0], s, j).wait_recv()
-            each_peer(rxl, xl.at[rows], 0, lambda c: c.start())
-            xl[rows, :] = rxl[...]
-
-            @pl.when(even)
-            def _():
-                to(sx, rxu, s_send.at[7], rx_recv.at[1], s, j).wait_recv()
-                each_peer(rxu, xu.at[rows], 1, lambda c: c.start())
-                xu[rows, :] = rxu[...]
+            to(sx0, xl.at[half_rows], s_send.at[2], rx_recv.at[0], s, j).wait_recv()
+            hand_xl().start()
+
+        @pl.when(even & (s > 0))
+        def _():
+            to(sx, xu.at[half_rows], s_send.at[7], rx_recv.at[1], s, j).wait_recv()
+            hand_xu().start()
 
     def fill():
         @pl.when(s > 0)
         def _():
-            each_peer(rxl, xl.at[rows], 0, lambda c: c.wait_recv())
+            hand_xl().wait_recv()
 
             @pl.when(even)
             def _():
-                each_peer(rxu, xu.at[rows], 1, lambda c: c.wait_recv())
+                hand_xu().wait_recv()
 
             xcat[0:N, :] = xl[...]
             xcat[N : 2 * N, :] = xu[...]
@@ -326,8 +377,9 @@
         xcat[2 * N : 2 * N + 8, :] = own_h[...]
 
     factor_start(d2, begin, f1b)
-    take_last(take_rest)
-    factor_rest(d2, fill, xcat, v2, ycat, f1b, f2b, zb, [(0, pl1), (N, pu1)])
+    hand_rest().wait_recv()
+    d2[other_rows, :] = dsib[...]
+    factor_rest(d2, pass_on, fill, xcat, v2, ycat, f1b, f2b, zb, [(0, pl1), (N, pu1)])
 
     own_level = []
     to_lower = jnp.bool_(False)
@@ -361,34 +413,34 @@
 
             @pl.when(mine & (lax.rem(s - d, 4 * d) == 2 * d))
             def _():
-                act(to(sx, rxu, s_send.at[7], rx_recv.at[1], s - d, j))
+                act(to(sx, xu.at[half_rows], s_send.at[7], rx_recv.at[1], s - d, j))
 
             @pl.when(mine & (s + d < 64) & (lax.rem(s + d, 4 * d) == 2 * d))
             def _():
-                act(to(sx, rxl, s_send.at[7], rx_recv.at[0], s + d, j))
+                act(to(sx, xl.at[half_rows], s_send.at[7], rx_recv.at[0], s + d, j))
 
     lead_sends(lambda c: c.start())
     finish_rows(v2, ycat, f2b, [0, N])
 
+    @pl.when(s > 0)
+    def _():
+        pl2[0:Q, :] = nt(v2[own_rows, :], v2[0:N, :])
+        pu2[0:Q, :] = nt(v2[pl.ds(own_at + N, Q), :], v2[N : 2 * N, :])
+        back = nt(v2[2 * N : 2 * N + 8, :], v2[0 : 2 * N, :])
+        pl2[Q : Q + 8, :] = back[:, 0:N]
+        pu2[Q : Q + 8, :] = back[:, N : 2 * N]
+
+    rest_sends(lambda c: c.start())
+
     @pl.when(to_lower)
     def _():
-        sx[...] = -nt(v2[pl.ds(start + N, 32), :], v2[0:N, :])
+        sx[...] = -nt(v2[pl.ds(half_at + N, H), :], v2[0:N, :])
 
     @pl.when(jnp.logical_not(to_lower) & (s > 0))
     def _():
-        sx[...] = -nt(v2[pl.ds(start, 32), :], v2[N : 2 * N, :])
+        sx[...] = -nt(v2[pl.ds(half_at, H), :], v2[N : 2 * N, :])
 
     link_sends(lambda c: c.start())
-
-    @pl.when(s > 0)
-    def _():
-        pl2[0:H, :] = nt(v2[H:N, :], v2[0:N, :])
-        pu2[0:H, :] = nt(v2[N + H : 2 * N, :], v2[N : 2 * N, :])
-        back = nt(v2[2 * N : 2 * N + 8, :], v2[0 : 2 * N, :])
-        pl2[H : H + 8, :] = back[:, 0:N]
-        pu2[H : H + 8, :] = back[:, N : 2 * N]
-
-    rest_sends(lambda c: c.start())
 
     @pl.when(s > 0)
     def _():
@@ -471,20 +523,25 @@
         def _():
             out[...] = both[:, 32 * i : 32 * i + 32]
 
-    for a in range(1, 5):
-        gather(a, lambda c: c.wait_send())
+    gather(3, lambda c: c.wait_send())
+    for a in (1, 2, 4):
+        direct(a, lambda c: c.wait_send())
+    for a in (1, 2):
+        hand_on(a, lambda c: c.wait_send())
 
     up0_sends(lambda c: c.wait_send())
     up0_link(lambda c: c.wait_send())
     up0_rest(lambda c: c.wait_send())
 
+    hand_rest().wait_send()
+
     @pl.when(s > 0)
     def _():
-        each_peer(rxl, xl.at[rows], 0, lambda c: c.wait_send())
-
-        @pl.when(even)
-        def _():
-            each_peer(rxu, xu.at[rows], 1, lambda c: c.wait_send())
+        hand_xl().wait_send()
+
+    @pl.when(even & (s > 0))
+    def _():
+        hand_xu().wait_send()
 
     lead_sends(lambda c: c.wait_send())
     link_sends(lambda c: c.wait_send())
@@ -500,8 +557,8 @@
     square = vmem((N, N), F32)
     half = vmem((H, H), F32)
     tall = vmem((2 * N + 8, N), F32)
-    slab = vmem((H + 8, N), F32)
-    slice_ = vmem((32, N), F32)
+    slab = vmem((Q + 8, N), F32)
+    wide = vmem((H, N), F32)
     return pl.pallas_call(
         kernel,
         out_shape=jax.ShapeDtypeStruct((2, 32), F32),
@@ -510,10 +567,10 @@
         scratch_shapes=[
             square, square, square, vmem((64, N), F32), square, square, square, tall, vmem((2 * N + 8, H), F32), tall, tall,
             half, half, half, half, half, half, tall, tall,
-            vmem((8, N), F32), vmem((13, H, H), F32), vmem((13, H + 8, N), F32),
-            slice_, slice_, half, slab, slice_, half, slab, half, slab, slice_,
+            vmem((8, N), F32), vmem((13, H, H), F32), vmem((13, Q + 8, N), F32), vmem((Q, N), F32),
+            half, slab, wide, half, slab, half, slab, wide,
             vmem((3, 8, N), F32), vmem((8, N), F32),
-            dma((5, 8)), dma((5, 8)), dma((2, 8)), dma((2, 8)),
+            dma((5, 8)), dma((5, 8)), dma((3,)), dma((3,)),
             dma((13,)), dma((13,)), dma((2,)), dma((8,)), dma((13,)), dma((3,)), dma((5,)),
         ],
         compiler_params=pltpu.CompilerParams(

time: 166 us -> 160 us (0.964)
  Pallas kernels: 163 us -> 157 us
    pallas_call x1, Pallas kernels: 163 us -> 157 us  [body(): pl.pallas_call(kernel, out_shape=jax.ShapeDtypeStruct((2, 32), F32), in_s...]
where the time goes in v4:
time: 160 us
  Pallas kernels  157 us (98%)
  local copies, waits for them, and re-layouts  3.15 us (2%)
    pallas_call x1, Pallas kernels, body(): pl.pallas_call(kernel, out_shape=jax.ShapeDtypeStruct((2, 32), F32), in_s...  157 us

profile of v4, /device:TPU:16, one launch (start us, length us, event | category | flops | bytes accessed | tf_op | source)
XLA Modules:
  0.0 160.1 jit_solution(8136572471462176491)
XLA Ops:
  0.0 0.0 copy-start.2
  0.0 0.7 copy-done.2
  0.7 0.2 dynamic_update_slice.3.info
  0.9 0.0 copy-start
  0.9 0.8 copy-done
  1.8 0.0 copy-start.1
  1.8 0.8 copy-done.1
  2.6 156.9 %shard_map.37 = f32[2,32]{1,0:T(2,128)S(1)} custom-call(f32[2,32,256]{2,1,0:T(8,128)S(1)} %copy-done, f32[2,32,256]{2,1,0:T(8,128)S(1)} %copy-done.1, f32[8,256]{1,0:T(8,128)S(1)} %dynamic_update_slice.3.info), custom_call_target="tpu_custom_call" | custom-call | tf_op jit(solution)/shard_map/pallas_call | solution.py:562
  159.5 0.6 copy.6
  (1 shorter events, 0.0 us)
Async XLA Ops:
  0.0 0.7 copy-start.2
  0.9 0.8 copy-start
  1.8 0.8 copy-start.1

commit v5 on v4

v5 whole, which is shorter than its diff:
```python
import jax
import jax.numpy as jnp
from jax import lax
from jax.experimental import pallas as pl
from jax.experimental.pallas import tpu as pltpu
from jax.sharding import PartitionSpec as P

N = 256
H = 128
Q = 64
F32 = jnp.float32
MESH = pl.DeviceIdType.MESH
EXACT = lax.Precision.HIGHEST


def nt(a, b):
    return lax.dot_general(
        a, b, (((1,), (1,)), ((), ())), precision=EXACT, preferred_element_type=F32
    )


def nn(a, b):
    return jnp.dot(a, b, precision=EXACT, preferred_element_type=F32)


def row_of(x, k):
    return jnp.broadcast_to(x[k : k + 1, :], x.shape)


def lane_of(x, l):
    return jnp.take_along_axis(x, jnp.full((8, H), l, jnp.int32), axis=1)


def sum8(t):
    return ((t[0] + t[1]) + (t[2] + t[3])) + ((t[4] + t[5]) + (t[6] + t[7]))


def pivot_block(w, b, sub, lane):
    at = 8 * b
    c = [lane_of(w[b], at + j) for j in range(8)]
    inside = (lane >= at) & (lane < at + 8)
    r = jnp.where(inside, (lane - at == sub).astype(F32), w[b])
    t = r
    pivots = jnp.ones((8, H), F32)
    inverses = []
    for k in range(0, 8, 2):
        first, second = sub == k, sub == k + 1
        p, q, o = row_of(c[k], k), row_of(c[k + 1], k), row_of(c[k + 1], k + 1)
        det = 1.0 / (p * o - q * q)
        m0 = jnp.where(first | second, 0.0, c[k])
        m1 = jnp.where(first | second, 0.0, c[k + 1])
        f0 = (m0 * o - m1 * q) * det
        f1 = (m1 * p - m0 * q) * det
        inverses.append((o * det, -q * det, p * det))
        ratio = q * (1.0 / p)
        r0, r1 = row_of(r, k), row_of(r, k + 1)
        t = jnp.where(first, r0, jnp.where(second, r1 - ratio * r0, t))
        pivots = jnp.where(first, p, jnp.where(second, o - ratio * q, pivots))
        for j in range(k + 2, 8):
            c[j] = c[j] - (f0 * row_of(c[j], k) + f1 * row_of(c[j], k + 1))
        r = r - (f0 * r0 + f1 * r1)
    if b < 15:
        rows = []
        for k in range(0, 8, 2):
            ia, ib, ic = inverses[k // 2]
            r0, r1 = row_of(r, k), row_of(r, k + 1)
            rows += [ia * r0 + ib * r1, ib * r0 + ic * r1]
        for i in range(b + 1, 16):
            cols = [lane_of(w[i], at + j) for j in range(8)]
            w[i] = jnp.where(inside, 0.0, w[i]) - sum8([cols[j] * rows[j] for j in range(8)])
    return jnp.where(lane < at + 8, t * lax.rsqrt(pivots), 0.0)


def factor_part(w, blocks):
    sub = lax.broadcasted_iota(jnp.int32, (8, H), 0)
    lane = lax.broadcasted_iota(jnp.int32, (8, H), 1)
    return [pivot_block(w, b, sub, lane) for b in blocks]


def groups(a):
    return [a[8 * r : 8 * r + 8, :] for r in range(16)]


def factor_start(block, begin, f1):
    w = groups(block[0:H, 0:H])
    out = factor_part(w, range(8))
    begin()
    out += factor_part(w, range(8, 16))
    f1[...] = jnp.concatenate(out, axis=0)


def factor_rest(block, steps, f1, f2, z):
    z[...] = nt(block[H:N, 0:H], f1[...])
    w = groups(block[H:N, H:N] - nt(z[...], z[...]))
    out = []
    for b in range(16):
        if b in steps:
            steps[b]()
        out += factor_part(w, [b])
    f2[...] = jnp.concatenate(out, axis=0)


def project(x, at, v, y, to, n, f1, z):
    v[to : to + n, 0:H] = nt(x[at : at + n, 0:H], f1[...])
    y[to : to + n, :] = x[at : at + n, H:N] - nt(v[to : to + n, 0:H], z[...])


def lead_start(v, to, at):
    to[...] = nt(v[at : at + H, 0:H], v[at : at + H, 0:H])


def lead_end(v, y, f2, to, at):
    top = nt(y[at : at + H, :], f2[...])
    v[at : at + H, H:N] = top
    to[...] = to[...] + nt(top, top)


def rest_rows(v, own, cols):
    return jnp.concatenate([v[own, cols], v[2 * N : 2 * N + 8, cols]], axis=0)


def rest_start(v, to, own, at):
    c = slice(0, H)
    to[...] = nt(rest_rows(v, own, c), v[at : at + N, c])


def rest_end(v, to, own, at):
    c = slice(H, N)
    to[...] = to[...] + nt(rest_rows(v, own, c), v[at : at + N, c])


def finish_rows(v, y, f2, at, n):
    v[at : at + n, H:N] = nt(y[at : at + n, :], f2[...])


def means(v, f1, f2, z):
    hi = nn(v[:, H:N], f2[...])
    lo = nn(v[:, 0:H] - nn(hi, z[...]), f1[...])
    return lo, hi


def kernel(
    diag, coup, info, out,
    d1, c0, c1, hin, d2, xl, xu, c1t, h1, ycat, v1, v2, f1a, f2a, za, f1b, f2b, zb, ga, gb,
    own_h, rc1, rc2, dsib, pu01, pu02, sx0, pl1, pl2, pu1, pu2, sx, xin, xown,
    g1_send, g1_recv, sib_send, sib_recv, r1_recv, r2_recv, rx_recv, s_send, x_send, x_recv, own_sem,
):
    s = lax.axis_index("tm")
    j = lax.axis_index("state")
    core = lax.rem(j, 2)
    sibling = j + 1 - 2 * core
    rows = pl.ds(pl.multiple_of(j * 32, 32), 32)
    own_rows = pl.ds(pl.multiple_of(H + core * Q, Q), Q)
    other_rows = pl.ds(pl.multiple_of(H + Q - core * Q, Q), Q)

    even = lax.rem(s, 2) == 0

    level, dist = jnp.int32(6), jnp.int32(64)
    to_lower, to_upper = jnp.bool_(False), jnp.bool_(False)
    for k in range(6):
        d = 2**k
        mine = lax.rem(s, 2 * d) == d
        level, dist = jnp.where(mine, k, level), jnp.where(mine, d, dist)
        if k < 5:
            to_lower = to_lower | (mine & (lax.rem(s - d, 4 * d) == 2 * d))
            to_upper = to_upper | (mine & (s + d < 64) & (lax.rem(s + d, 4 * d) == 2 * d))
    inner = s > 0
    upper = s + dist < 64

    barrier = pltpu.get_barrier_semaphore()
    for r in range(1, 8):
        pl.semaphore_signal(
            barrier, inc=1, device_id=(s, lax.rem(j + r, 8)), device_id_type=MESH
        )

    def greet(k, carry):
        d, count = carry
        up = s + d < 64

        @pl.when(inner)
        def _():
            pl.semaphore_signal(barrier, inc=1, device_id=(s - d, j), device_id_type=MESH)

        @pl.when(up)
        def _():
            pl.semaphore_signal(barrier, inc=1, device_id=(s + d, j), device_id_type=MESH)

        return 2 * d, count + inner.astype(jnp.int32) + up.astype(jnp.int32)

    _, count = lax.fori_loop(0, level + 1, greet, (jnp.int32(1), jnp.int32(7)))

    first = [
        (diag.at[1], d1.at[rows]),
        (coup.at[0], c0.at[rows]),
        (coup.at[1], c1.at[rows]),
        (info, hin.at[pl.ds(pl.multiple_of(j * 8, 8), 8)]),
        (diag.at[0], d2.at[rows]),
    ]
    local = [
        pltpu.make_async_copy(src, dst, own_sem.at[a]) for a, (src, dst) in enumerate(first)
    ]
    for c in local:
        c.start()

    @pl.when(s == 0)
    def _():
        xl[...] = jnp.zeros((N, N), F32)
        xu[...] = jnp.zeros((N, N), F32)

    pl.semaphore_wait(barrier, count)

    def to(src, dst, send, recv, tm, state):
        return pltpu.make_async_remote_copy(
            src_ref=src, dst_ref=dst, send_sem=send, recv_sem=recv,
            device_id=(tm, state), device_id_type=MESH,
        )

    def peer(src, dst, sends, recvs, a, r):
        return to(src, dst, sends.at[a, r], recvs.at[a, r], s, lax.rem(j + r, 8))

    def gather(a, act):
        src, dst = first[a]
        for r in range(1, 8):
            act(peer(src, dst, g1_send, g1_recv, a, r))

    def direct(a, act):
        src, dst = first[a]
        for r in (2, 4, 6):
            act(peer(src, dst, g1_send, g1_recv, a, r))
        act(to(src, dst, g1_send.at[a, 1], g1_recv.at[a, 1], s, sibling))

    def hand_on(a, act):
        whole = (None, c0, c1, None, d2)[a]
        for r in (2, 4, 6):
            at = pl.ds(pl.multiple_of(lax.rem(j + 8 - r, 8) * 32, 32), 32)
            piece = whole.at[at]
            act(to(piece, piece, g1_send.at[a, r + 1], g1_recv.at[a, r + 1], s, sibling))

    def direct_arrived(a):
        src, dst = first[a]
        for r in (2, 4, 6):
            peer(src, dst, g1_send, g1_recv, a, r).wait_recv()

    def arrived(a):
        src, dst = first[a]
        local[a].wait()
        to(src, dst, g1_send.at[a, 1], g1_recv.at[a, 1], s, sibling).wait_recv()
        hand_on(a, lambda c: c.wait_recv())

    gather(0, lambda c: c.start())
    gather(0, lambda c: c.wait_send())
    for a in (1, 2, 4):
        direct(a, lambda c: c.start())
    gather(3, lambda c: c.start())

    local[0].wait()
    gather(0, lambda c: c.wait_recv())
    factor_start(d1, lambda: None, f1a)

    def pass_on0():
        for a in (1, 2):
            direct_arrived(a)
            hand_on(a, lambda c: c.start())

    def fill0():
        direct_arrived(4)
        hand_on(4, lambda c: c.start())
        arrived(1)
        arrived(2)
        local[3].wait()
        gather(3, lambda c: c.wait_recv())
        info_all = sum8([hin[8 * i : 8 * i + 8, :] for i in range(8)])
        own_h[...] = row_of(info_all, 0)
        h1[...] = row_of(info_all, 1)
        c1t[...] = jnp.where(s == 63, 0.0, c1[...].T)
        project(c1t, 0, v1, ycat, N, H, f1a, za)
        lead_start(v1, pu01, N)
        project(c1t, H, v1, ycat, N + H, H, f1a, za)
        project(h1, 0, v1, ycat, 2 * N, 8, f1a, za)
        rest_start(v1, pu02, up_rows, N)
        project(c0, 0, v1, ycat, 0, N, f1a, za)

    up_rows = pl.ds(pl.multiple_of(N + H + core * Q, Q), Q)
    factor_rest(d1, {2: pass_on0, 12: fill0}, f1a, f2a, za)
    lead_end(v1, ycat, f2a, pu01, N)

    up0 = s < 63

    def up0_sends(act):
        @pl.when(up0)
        def _():
            act(to(pu01, rc1.at[0], s_send.at[0], r1_recv.at[0], s + 1, j))

    def up0_rest(act):
        @pl.when(up0)
        def _():
            act(to(pu02, rc2.at[0], s_send.at[1], r2_recv.at[0], s + 1, j))

    def part_rows(part):
        return pl.ds(pl.multiple_of(part * H + core * Q, Q), Q)

    def part_of(v, part, base):
        return v[pl.ds(pl.multiple_of(base + part * H + core * Q, Q), Q), :]

    def up0_link(act):
        @pl.when(even)
        def _():
            for part in range(2):
                act(to(sx0.at[part], xl.at[part_rows(part)], s_send.at[2 + part], rx_recv.at[0, part], s + 1, j))

    up0_sends(lambda c: c.start())
    finish_rows(v1, ycat, f2a, N + H, H)
    finish_rows(v1, ycat, f2a, 2 * N, 8)
    rest_end(v1, pu02, up_rows, N)
    up0_rest(lambda c: c.start())
    finish_rows(v1, ycat, f2a, 0, N)
    for part in range(2):
        sx0[part] = -nt(part_of(v1, part, 0), v1[N : 2 * N, :])
    up0_link(lambda c: c.start())
    back = nt(v1[2 * N : 2 * N + 8, :], v1[0:N, :])
    own_h[...] = own_h[...] - back
    arrived(4)
    hand_on(4, lambda c: c.wait_send())
    d2[0:H, 0:H] = d2[0:H, 0:H] - nt(v1[0:H, :], v1[0:H, :])
    d2[own_rows, :] = d2[own_rows, :] - nt(v1[own_rows, :], v1[0:N, :])

    @pl.when(jnp.logical_not(even))
    def _():
        xu[...] = -nt(v1[N : 2 * N, :], v1[0:N, :])

    def take_lead(slot):
        to(pl1, rc1.at[slot], s_send.at[4], r1_recv.at[slot], s, j).wait_recv()
        d2[0:H, 0:H] = d2[0:H, 0:H] - rc1[slot]

    def take_rest(slot):
        to(pl2, rc2.at[slot], s_send.at[5], r2_recv.at[slot], s, j).wait_recv()
        d2[own_rows, :] = d2[own_rows, :] - rc2[slot, 0:Q, :]
        own_h[...] = own_h[...] - rc2[slot, Q : Q + 8, :]

    @pl.when(even & inner)
    def _():
        take_lead(0)
        take_rest(0)

    def early(k, carry):
        @pl.when(inner)
        def _():
            take_lead(1 + 2 * k)
            take_rest(1 + 2 * k)

        take_lead(2 + 2 * k)
        take_rest(2 + 2 * k)
        return carry

    lax.fori_loop(0, jnp.maximum(level - 1, 0), early, 0)

    left_slot = jnp.where(even, 2 * level - 1, 0)

    def take_last(take):
        @pl.when(inner)
        def _():
            take(left_slot)

        @pl.when(even)
        def _():
            take(2 * level)

    take_last(take_lead)

    def hand(ref_rows, dst, a):
        return to(ref_rows, dst, sib_send.at[a], sib_recv.at[a], s, sibling)

    def hand_rest():
        return hand(d2.at[own_rows], dsib, 0)

    def hand_link(x, part, a):
        return hand(x.at[part_rows(part)], x.at[part_rows(part)], 1 + 2 * a + part)

    def begin():
        take_last(take_rest)
        hand_rest().start()

    def pass_on(part):
        @pl.when(inner)
        def _():
            to(sx0.at[0], xl.at[part_rows(part)], s_send.at[2], rx_recv.at[0, part], s, j).wait_recv()
            hand_link(xl, part, 0).start()

        @pl.when(even & inner)
        def _():
            to(sx0.at[0], xu.at[part_rows(part)], s_send.at[2], rx_recv.at[1, part], s, j).wait_recv()
            hand_link(xu, part, 1).start()

    def handed(part, act):
        @pl.when(inner)
        def _():
            act(hand_link(xl, part, 0))

        @pl.when(even & inner)
        def _():
            act(hand_link(xu, part, 1))

    def fill_lead():
        handed(0, lambda c: c.wait_recv())
        for x, at, to_ in ((xl, 0, pl1), (xu, N, pu1)):
            project(x, 0, v2, ycat, at, H, f1b, zb)
            lead_start(v2, to_, at)

    def fill_rest():
        handed(1, lambda c: c.wait_recv())
        project(own_h, 0, v2, ycat, 2 * N, 8, f1b, zb)
        for x, at, to_, own in ((xl, 0, pl2, own_rows), (xu, N, pu2, up_rows)):
            project(x, H, v2, ycat, at + H, H, f1b, zb)
            rest_start(v2, to_, own, at)

    factor_start(d2, begin, f1b)
    hand_rest().wait_recv()
    d2[other_rows, :] = dsib[...]
    steps = {1: lambda: pass_on(0), 3: lambda: pass_on(1), 6: fill_lead, 12: fill_rest}
    factor_rest(d2, steps, f1b, f2b, zb)
    lead_end(v2, ycat, f2b, pl1, 0)
    lead_end(v2, ycat, f2b, pu1, N)

    lower_slot, upper_slot = 2 + 2 * level, 1 + 2 * level

    def lead_sends(act):
        @pl.when(inner)
        def _():
            act(to(pl1, rc1.at[lower_slot], s_send.at[4], r1_recv.at[lower_slot], s - dist, j))

        @pl.when(upper)
        def _():
            act(to(pu1, rc1.at[upper_slot], s_send.at[5], r1_recv.at[upper_slot], s + dist, j))

    def rest_sends(act):
        @pl.when(inner)
        def _():
            act(to(pl2, rc2.at[lower_slot], s_send.at[6], r2_recv.at[lower_slot], s - dist, j))

        @pl.when(upper)
        def _():
            act(to(pu2, rc2.at[upper_slot], s_send.at[7], r2_recv.at[upper_slot], s + dist, j))

    def link_send(part, act):
        at = part_rows(part)

        @pl.when(to_lower)
        def _():
            act(to(sx.at[part], xu.at[at], s_send.at[8 + part], rx_recv.at[1, part], s - dist, j))

        @pl.when(to_upper)
        def _():
            act(to(sx.at[part], xl.at[at], s_send.at[8 + part], rx_recv.at[0, part], s + dist, j))

    lead_sends(lambda c: c.start())
    for at in (H, N + H):
        finish_rows(v2, ycat, f2b, at, H)
    finish_rows(v2, ycat, f2b, 2 * N, 8)
    rest_end(v2, pl2, own_rows, 0)
    rest_end(v2, pu2, up_rows, N)
    rest_sends(lambda c: c.start())

    for part in range(2):

        @pl.when(to_lower)
        def _():
            sx[part] = -nt(part_of(v2, part, N), v2[0:N, :])

        @pl.when(to_upper)
        def _():
            sx[part] = -nt(part_of(v2, part, 0), v2[N : 2 * N, :])

        link_send(part, lambda c: c.start())

    @pl.when(inner)
    def _():
        lo, hi = means(v2, f1b, f2b, zb)
        gb[:, 0:H] = lo
        gb[:, H:N] = hi

    def early_means():
        lo, hi = means(v1, f1a, f2a, za)
        ga[:, 0:H] = lo
        ga[:, H:N] = hi

    @pl.when(s > 0)
    def _():
        early_means()

    @pl.when(inner)
    def _():
        to(xown, xin.at[0], x_send.at[0], x_recv.at[0], s, j).wait_recv()

    @pl.when(upper)
    def _():
        to(xown, xin.at[1], x_send.at[0], x_recv.at[1], s, j).wait_recv()

    @pl.when(jnp.logical_not(upper))
    def _():
        xin[1] = jnp.zeros((8, N), F32)

    @pl.when(s == 0)
    def _():
        lo, hi = means(v2[2 * N : 2 * N + 8, :], f1b, f2b, zb)
        xown[:, 0:H] = lo
        xown[:, H:N] = hi

    @pl.when(s > 0)
    def _():
        xown[...] = gb[2 * N : 2 * N + 8, :] - (
            nn(xin[0], gb[0:N, :]) + nn(xin[1], gb[N : 2 * N, :])
        )

    def spread(act):
        def step(i, d):
            k = level - 1 - i
            act(to(xown, xin.at[0], x_send.at[2 * k], x_recv.at[0], s + d, j))

            @pl.when(inner)
            def _():
                act(to(xown, xin.at[1], x_send.at[2 * k + 1], x_recv.at[1], s - d, j))

            return d // 2

        lax.fori_loop(0, level, step, dist // 2)

        @pl.when(jnp.logical_not(even))
        def _():
            act(to(xown, xin.at[2], x_send.at[12], x_recv.at[2], s - 1, j))

    spread(lambda c: c.start())

    @pl.when(s == 0)
    def _():
        early_means()

    part = ga[2 * N : 2 * N + 8, :] - nn(xown[...], ga[0:N, :])

    @pl.when(even)
    def _():
        to(xown, xin.at[2], x_send.at[12], x_recv.at[2], s, j).wait_recv()

    @pl.when(jnp.logical_not(even))
    def _():
        xin[2] = xin[1]

    later = part - nn(xin[2], ga[N : 2 * N, :])
    both = jnp.concatenate([xown[0:1, :], later[0:1, :]], axis=0)
    for i in range(8):

        @pl.when(j == i)
        def _():
            out[...] = both[:, 32 * i : 32 * i + 32]

    gather(3, lambda c: c.wait_send())
    for a in (1, 2, 4):
        direct(a, lambda c: c.wait_send())
    for a in (1, 2):
        hand_on(a, lambda c: c.wait_send())

    up0_sends(lambda c: c.wait_send())
    up0_link(lambda c: c.wait_send())
    up0_rest(lambda c: c.wait_send())

    hand_rest().wait_send()

    for part in range(2):
        handed(part, lambda c: c.wait_send())

    lead_sends(lambda c: c.wait_send())
    for part in range(2):
        link_send(part, lambda c: c.wait_send())
    rest_sends(lambda c: c.wait_send())
    spread(lambda c: c.wait_send())


def body(diagonal, coupling, info):
    offset = lax.axis_index("state") * 32
    placed = lax.dynamic_update_slice(jnp.zeros((8, N), F32), info, (0, offset))
    vmem = pltpu.VMEM
    dma = pltpu.SemaphoreType.DMA
    square = vmem((N, N), F32)
    half = vmem((H, H), F32)
    tall = vmem((2 * N + 8, N), F32)
    slab = vmem((Q + 8, N), F32)
    pair = vmem((2, Q, N), F32)
    return pl.pallas_call(
        kernel,
        out_shape=jax.ShapeDtypeStruct((2, 32), F32),
        in_specs=[pl.BlockSpec(memory_space=pltpu.HBM)] * 3,
        out_specs=pl.BlockSpec(memory_space=vmem),
        scratch_shapes=[
            square, square, square, vmem((64, N), F32), square, square, square, square, vmem((8, N), F32), vmem((2 * N + 8, H), F32), tall, tall,
            half, half, half, half, half, half, tall, tall,
            vmem((8, N), F32), vmem((13, H, H), F32), vmem((13, Q + 8, N), F32), vmem((Q, N), F32),
            half, slab, pair, half, slab, half, slab, pair,
            vmem((3, 8, N), F32), vmem((8, N), F32),
            dma((5, 8)), dma((5, 8)), dma((5,)), dma((5,)),
            dma((13,)), dma((13,)), dma((2, 2)), dma((10,)), dma((13,)), dma((3,)), dma((5,)),
        ],
        compiler_params=pltpu.CompilerParams(
            collective_id=0, has_side_effects=True, vmem_limit_bytes=32 * 1024 * 1024
        ),
    )(diagonal, coupling, placed)


def solution(mesh):
    placed = (P("tm", "state", None), P("tm", "state", None), P("tm", "state"))
    return jax.shard_map(
        body, mesh=mesh, in_specs=placed, out_specs=P("tm", "state"), check_vma=False
    )
```

time: 160 us -> 157 us (0.981)
  Pallas kernels: 157 us -> 154 us
    pallas_call x1, Pallas kernels: 157 us -> 154 us  [body(): pl.pallas_call(kernel, out_shape=jax.ShapeDtypeStruct((2, 32), F32), in_s...]
where the time goes in v5:
time: 157 us
  Pallas kernels  154 us (98%)
  local copies, waits for them, and re-layouts  3.15 us (2%)
    pallas_call x1, Pallas kernels, body(): pl.pallas_call(kernel, out_shape=jax.ShapeDtypeStruct((2, 32), F32), in_s...  154 us

profile of v5, /device:TPU:16, one launch (start us, length us, event | category | flops | bytes accessed | tf_op | source)
XLA Modules:
  0.0 156.9 jit_solution(16771757009448022313)
XLA Ops:
  0.0 0.0 copy-start.2
  0.0 0.7 copy-done.2
  0.7 0.2 dynamic_update_slice.3.info
  0.9 0.0 copy-start
  0.9 0.8 copy-done
  1.8 0.0 copy-start.1
  1.8 0.8 copy-done.1
  2.6 153.8 %shard_map.37 = f32[2,32]{1,0:T(2,128)S(1)} custom-call(f32[2,32,256]{2,1,0:T(8,128)S(1)} %copy-done, f32[2,32,256]{2,1,0:T(8,128)S(1)} %copy-done.1, f32[8,256]{1,0:T(8,128)S(1)} %dynamic_update_slice.3.info), custom_call_target="tpu_custom_call" | custom-call | tf_op jit(solution)/shard_map/pallas_call | solution.py:587
  156.4 0.6 copy.6
  (1 shorter events, 0.0 us)
Async XLA Ops:
  0.0 0.7 copy-start.2
  0.9 0.8 copy-start
  1.8 0.8 copy-start.1

commit v6 on v5

--- a/solution.py
+++ b/solution.py
@@ -7,7 +7,6 @@
 
 N = 256
 H = 128
-Q = 64
 F32 = jnp.float32
 MESH = pl.DeviceIdType.MESH
 EXACT = lax.Precision.HIGHEST
@@ -81,12 +80,8 @@
     return [a[8 * r : 8 * r + 8, :] for r in range(16)]
 
 
-def factor_start(block, begin, f1):
-    w = groups(block[0:H, 0:H])
-    out = factor_part(w, range(8))
-    begin()
-    out += factor_part(w, range(8, 16))
-    f1[...] = jnp.concatenate(out, axis=0)
+def factor_start(block, f1):
+    f1[...] = jnp.concatenate(factor_part(groups(block[0:H, 0:H]), range(16)), axis=0)
 
 
 def factor_rest(block, steps, f1, f2, z):
@@ -115,18 +110,9 @@
     to[...] = to[...] + nt(top, top)
 
 
-def rest_rows(v, own, cols):
-    return jnp.concatenate([v[own, cols], v[2 * N : 2 * N + 8, cols]], axis=0)
-
-
-def rest_start(v, to, own, at):
-    c = slice(0, H)
-    to[...] = nt(rest_rows(v, own, c), v[at : at + N, c])
-
-
-def rest_end(v, to, own, at):
-    c = slice(H, N)
-    to[...] = to[...] + nt(rest_rows(v, own, c), v[at : at + N, c])
+def rest_products(v, to, at):
+    to[0:H, :] = nt(v[at + H : at + N, :], v[at : at + N, :])
+    to[H : H + 8, :] = nt(v[2 * N : 2 * N + 8, :], v[at : at + N, :])
 
 
 def finish_rows(v, y, f2, at, n):
@@ -142,16 +128,14 @@
 def kernel(
     diag, coup, info, out,
     d1, c0, c1, hin, d2, xl, xu, c1t, h1, ycat, v1, v2, f1a, f2a, za, f1b, f2b, zb, ga, gb,
-    own_h, rc1, rc2, dsib, pu01, pu02, sx0, pl1, pl2, pu1, pu2, sx, xin, xown,
-    g1_send, g1_recv, sib_send, sib_recv, r1_recv, r2_recv, rx_recv, s_send, x_send, x_recv, own_sem,
+    own_h, rc1, rc2, pu01, pu02, sx0, pl1, pl2, pu1, pu2, sx, xin, xown,
+    g1_send, g1_recv, r1_recv, r2_recv, rx_recv, s_send, x_send, x_recv, own_sem,
 ):
     s = lax.axis_index("tm")
     j = lax.axis_index("state")
     core = lax.rem(j, 2)
     sibling = j + 1 - 2 * core
     rows = pl.ds(pl.multiple_of(j * 32, 32), 32)
-    own_rows = pl.ds(pl.multiple_of(H + core * Q, Q), Q)
-    other_rows = pl.ds(pl.multiple_of(H + Q - core * Q, Q), Q)
 
     even = lax.rem(s, 2) == 0
 
@@ -190,11 +174,12 @@
     _, count = lax.fori_loop(0, level + 1, greet, (jnp.int32(1), jnp.int32(7)))
 
     first = [
-        (diag.at[1], d1.at[rows]),
+        (diag.at[1, :, 0:H], d1.at[rows, 0:H]),
         (coup.at[0], c0.at[rows]),
         (coup.at[1], c1.at[rows]),
         (info, hin.at[pl.ds(pl.multiple_of(j * 8, 8), 8)]),
         (diag.at[0], d2.at[rows]),
+        (diag.at[1, :, H:N], d1.at[rows, H:N]),
     ]
     local = [
         pltpu.make_async_copy(src, dst, own_sem.at[a]) for a, (src, dst) in enumerate(first)
@@ -248,27 +233,29 @@
         hand_on(a, lambda c: c.wait_recv())
 
     gather(0, lambda c: c.start())
+    gather(5, lambda c: c.start())
     gather(0, lambda c: c.wait_send())
-    for a in (1, 2, 4):
+    gather(5, lambda c: c.wait_send())
+    for a in (2, 1, 4):
         direct(a, lambda c: c.start())
     gather(3, lambda c: c.start())
 
-    local[0].wait()
-    gather(0, lambda c: c.wait_recv())
-    factor_start(d1, lambda: None, f1a)
-
-    def pass_on0():
-        for a in (1, 2):
-            direct_arrived(a)
-            hand_on(a, lambda c: c.start())
+    def gathered(a):
+        local[a].wait()
+        gather(a, lambda c: c.wait_recv())
+
+    gathered(0)
+    factor_start(d1, f1a)
+    gathered(5)
+
+    for a in (2, 1):
+        direct_arrived(a)
+        hand_on(a, lambda c: c.start())
 
     def fill0():
-        direct_arrived(4)
-        hand_on(4, lambda c: c.start())
+        arrived(2)
         arrived(1)
-        arrived(2)
-        local[3].wait()
-        gather(3, lambda c: c.wait_recv())
+        gathered(3)
         info_all = sum8([hin[8 * i : 8 * i + 8, :] for i in range(8)])
         own_h[...] = row_of(info_all, 0)
         h1[...] = row_of(info_all, 1)
@@ -277,11 +264,9 @@
         lead_start(v1, pu01, N)
         project(c1t, H, v1, ycat, N + H, H, f1a, za)
         project(h1, 0, v1, ycat, 2 * N, 8, f1a, za)
-        rest_start(v1, pu02, up_rows, N)
         project(c0, 0, v1, ycat, 0, N, f1a, za)
 
-    up_rows = pl.ds(pl.multiple_of(N + H + core * Q, Q), Q)
-    factor_rest(d1, {2: pass_on0, 12: fill0}, f1a, f2a, za)
+    factor_rest(d1, {12: fill0}, f1a, f2a, za)
     lead_end(v1, ycat, f2a, pu01, N)
 
     up0 = s < 63
@@ -297,10 +282,7 @@
             act(to(pu02, rc2.at[0], s_send.at[1], r2_recv.at[0], s + 1, j))
 
     def part_rows(part):
-        return pl.ds(pl.multiple_of(part * H + core * Q, Q), Q)
-
-    def part_of(v, part, base):
-        return v[pl.ds(pl.multiple_of(base + part * H + core * Q, Q), Q), :]
+        return pl.ds(part * H, H)
 
     def up0_link(act):
         @pl.when(even)
@@ -311,18 +293,20 @@
     up0_sends(lambda c: c.start())
     finish_rows(v1, ycat, f2a, N + H, H)
     finish_rows(v1, ycat, f2a, 2 * N, 8)
-    rest_end(v1, pu02, up_rows, N)
+    rest_products(v1, pu02, N)
     up0_rest(lambda c: c.start())
     finish_rows(v1, ycat, f2a, 0, N)
     for part in range(2):
-        sx0[part] = -nt(part_of(v1, part, 0), v1[N : 2 * N, :])
+        sx0[part] = -nt(v1[part * H : part * H + H, :], v1[N : 2 * N, :])
     up0_link(lambda c: c.start())
+    direct_arrived(4)
+    hand_on(4, lambda c: c.start())
     back = nt(v1[2 * N : 2 * N + 8, :], v1[0:N, :])
     own_h[...] = own_h[...] - back
     arrived(4)
     hand_on(4, lambda c: c.wait_send())
     d2[0:H, 0:H] = d2[0:H, 0:H] - nt(v1[0:H, :], v1[0:H, :])
-    d2[own_rows, :] = d2[own_rows, :] - nt(v1[own_rows, :], v1[0:N, :])
+    d2[H:N, :] = d2[H:N, :] - nt(v1[H:N, :], v1[0:N, :])
 
     @pl.when(jnp.logical_not(even))
     def _():
@@ -334,8 +318,8 @@
 
     def take_rest(slot):
         to(pl2, rc2.at[slot], s_send.at[5], r2_recv.at[slot], s, j).wait_recv()
-        d2[own_rows, :] = d2[own_rows, :] - rc2[slot, 0:Q, :]
-        own_h[...] = own_h[...] - rc2[slot, Q : Q + 8, :]
+        d2[H:N, :] = d2[H:N, :] - rc2[slot, 0:H, :]
+        own_h[...] = own_h[...] - rc2[slot, H : H + 8, :]
 
     @pl.when(even & inner)
     def _():
@@ -367,57 +351,26 @@
 
     take_last(take_lead)
 
-    def hand(ref_rows, dst, a):
-        return to(ref_rows, dst, sib_send.at[a], sib_recv.at[a], s, sibling)
-
-    def hand_rest():
-        return hand(d2.at[own_rows], dsib, 0)
-
-    def hand_link(x, part, a):
-        return hand(x.at[part_rows(part)], x.at[part_rows(part)], 1 + 2 * a + part)
-
-    def begin():
-        take_last(take_rest)
-        hand_rest().start()
-
-    def pass_on(part):
+    def take_link(part):
         @pl.when(inner)
         def _():
             to(sx0.at[0], xl.at[part_rows(part)], s_send.at[2], rx_recv.at[0, part], s, j).wait_recv()
-            hand_link(xl, part, 0).start()
 
         @pl.when(even & inner)
         def _():
             to(sx0.at[0], xu.at[part_rows(part)], s_send.at[2], rx_recv.at[1, part], s, j).wait_recv()
-            hand_link(xu, part, 1).start()
-
-    def handed(part, act):
-        @pl.when(inner)
-        def _():
-            act(hand_link(xl, part, 0))
-
-        @pl.when(even & inner)
-        def _():
-            act(hand_link(xu, part, 1))
-
-    def fill_lead():
-        handed(0, lambda c: c.wait_recv())
+
+    factor_start(d2, f1b)
+    take_last(take_rest)
+    take_link(0)
+
+    def fill():
+        project(own_h, 0, v2, ycat, 2 * N, 8, f1b, zb)
         for x, at, to_ in ((xl, 0, pl1), (xu, N, pu1)):
             project(x, 0, v2, ycat, at, H, f1b, zb)
             lead_start(v2, to_, at)
 
-    def fill_rest():
-        handed(1, lambda c: c.wait_recv())
-        project(own_h, 0, v2, ycat, 2 * N, 8, f1b, zb)
-        for x, at, to_, own in ((xl, 0, pl2, own_rows), (xu, N, pu2, up_rows)):
-            project(x, H, v2, ycat, at + H, H, f1b, zb)
-            rest_start(v2, to_, own, at)
-
-    factor_start(d2, begin, f1b)
-    hand_rest().wait_recv()
-    d2[other_rows, :] = dsib[...]
-    steps = {1: lambda: pass_on(0), 3: lambda: pass_on(1), 6: fill_lead, 12: fill_rest}
-    factor_rest(d2, steps, f1b, f2b, zb)
+    factor_rest(d2, {6: fill}, f1b, f2b, zb)
     lead_end(v2, ycat, f2b, pl1, 0)
     lead_end(v2, ycat, f2b, pu1, N)
 
@@ -453,22 +406,24 @@
             act(to(sx.at[part], xl.at[at], s_send.at[8 + part], rx_recv.at[0, part], s + dist, j))
 
     lead_sends(lambda c: c.start())
-    for at in (H, N + H):
+    take_link(1)
+    for x, at in ((xl, H), (xu, N + H)):
+        project(x, H, v2, ycat, at, H, f1b, zb)
         finish_rows(v2, ycat, f2b, at, H)
     finish_rows(v2, ycat, f2b, 2 * N, 8)
-    rest_end(v2, pl2, own_rows, 0)
-    rest_end(v2, pu2, up_rows, N)
+    rest_products(v2, pl2, 0)
+    rest_products(v2, pu2, N)
     rest_sends(lambda c: c.start())
 
     for part in range(2):
 
         @pl.when(to_lower)
         def _():
-            sx[part] = -nt(part_of(v2, part, N), v2[0:N, :])
+            sx[part] = -nt(v2[N + part * H : N + part * H + H, :], v2[0:N, :])
 
         @pl.when(to_upper)
         def _():
-            sx[part] = -nt(part_of(v2, part, 0), v2[N : 2 * N, :])
+            sx[part] = -nt(v2[part * H : part * H + H, :], v2[N : 2 * N, :])
 
         link_send(part, lambda c: c.start())
 
@@ -562,10 +517,6 @@
     up0_link(lambda c: c.wait_send())
     up0_rest(lambda c: c.wait_send())
 
-    hand_rest().wait_send()
-
-    for part in range(2):
-        handed(part, lambda c: c.wait_send())
 
     lead_sends(lambda c: c.wait_send())
     for part in range(2):
@@ -582,8 +533,8 @@
     square = vmem((N, N), F32)
     half = vmem((H, H), F32)
     tall = vmem((2 * N + 8, N), F32)
-    slab = vmem((Q + 8, N), F32)
-    pair = vmem((2, Q, N), F32)
+    slab = vmem((H + 8, N), F32)
+    pair = vmem((2, H, N), F32)
     return pl.pallas_call(
         kernel,
         out_shape=jax.ShapeDtypeStruct((2, 32), F32),
@@ -592,11 +543,11 @@
         scratch_shapes=[
             square, square, square, vmem((64, N), F32), square, square, square, square, vmem((8, N), F32), vmem((2 * N + 8, H), F32), tall, tall,
             half, half, half, half, half, half, tall, tall,
-            vmem((8, N), F32), vmem((13, H, H), F32), vmem((13, Q + 8, N), F32), vmem((Q, N), F32),
+            vmem((8, N), F32), vmem((13, H, H), F32), vmem((13, H + 8, N), F32),
             half, slab, pair, half, slab, half, slab, pair,
             vmem((3, 8, N), F32), vmem((8, N), F32),
-            dma((5, 8)), dma((5, 8)), dma((5,)), dma((5,)),
-            dma((13,)), dma((13,)), dma((2, 2)), dma((10,)), dma((13,)), dma((3,)), dma((5,)),
+            dma((6, 8)), dma((6, 8)),
+            dma((13,)), dma((13,)), dma((2, 2)), dma((10,)), dma((13,)), dma((3,)), dma((6,)),
         ],
         compiler_params=pltpu.CompilerParams(
             collective_id=0, has_side_effects=True, vmem_limit_bytes=32 * 1024 * 1024

time: 157 us -> 158 us (level)
  no operation moved by 1% of the time
where the time goes in v6:
time: 158 us; the launch traced here: 157 us
  Pallas kernels  154 us (97%)
  local copies, waits for them, and re-layouts  3.15 us (2%)
    pallas_call x1, Pallas kernels, body(): pl.pallas_call(kernel, out_shape=jax.ShapeDtypeStruct((2, 32), F32), in_s...  154 us

profile of v6, /device:TPU:16, one launch (start us, length us, event | category | flops | bytes accessed | tf_op | source)
XLA Modules:
  0.0 157.3 jit_solution(8964364715825344026)
XLA Ops:
  0.0 0.0 copy-start.2
  0.0 0.7 copy-done.2
  0.7 0.2 dynamic_update_slice.3.info
  0.9 0.0 copy-start
  0.9 0.8 copy-done
  1.8 0.0 copy-start.1
  1.8 0.8 copy-done.1
  2.6 154.1 %shard_map.37 = f32[2,32]{1,0:T(2,128)S(1)} custom-call(f32[2,32,256]{2,1,0:T(8,128)S(1)} %copy-done, f32[2,32,256]{2,1,0:T(8,128)S(1)} %copy-done.1, f32[8,256]{1,0:T(8,128)S(1)} %dynamic_update_slice.3.info), custom_call_target="tpu_custom_call" | custom-call | tf_op jit(solution)/shard_map/pallas_call | solution.py:538
  156.7 0.6 copy.6
  (1 shorter events, 0.0 us)
Async XLA Ops:
  0.0 0.7 copy-start.2
  0.9 0.8 copy-start
  1.8 0.8 copy-start.1

commit v7 on v6

--- a/solution.py
+++ b/solution.py
@@ -127,7 +127,7 @@
 
 def kernel(
     diag, coup, info, out,
-    d1, c0, c1, hin, d2, xl, xu, c1t, h1, ycat, v1, v2, f1a, f2a, za, f1b, f2b, zb, ga, gb,
+    d1, c0, c1, hin, d2, xl, xu, c1t, h1, ycat, v1, v2, f1a, f2a, za, f1b, f2b, zb, f1c, f2c, zc, hv, hy, xfirst, ga, gb,
     own_h, rc1, rc2, pu01, pu02, sx0, pl1, pl2, pu1, pu2, sx, xin, xown,
     g1_send, g1_recv, r1_recv, r2_recv, rx_recv, s_send, x_send, x_recv, own_sem,
 ):
@@ -172,6 +172,19 @@
         return 2 * d, count + inner.astype(jnp.int32) + up.astype(jnp.int32)
 
     _, count = lax.fori_loop(0, level + 1, greet, (jnp.int32(1), jnp.int32(7)))
+
+    root = s == 32
+    reads_first = (s == 1) | (s == 2) | (s == 4) | (s == 8)
+    count = count + reads_first.astype(jnp.int32) + 4 * root.astype(jnp.int32)
+
+    @pl.when(reads_first)
+    def _():
+        pl.semaphore_signal(barrier, inc=1, device_id=(32, j), device_id_type=MESH)
+
+    @pl.when(root)
+    def _():
+        for k in range(4):
+            pl.semaphore_signal(barrier, inc=1, device_id=(2**k, j), device_id_type=MESH)
 
     first = [
         (diag.at[1, :, 0:H], d1.at[rows, 0:H]),
@@ -186,11 +199,6 @@
     ]
     for c in local:
         c.start()
-
-    @pl.when(s == 0)
-    def _():
-        xl[...] = jnp.zeros((N, N), F32)
-        xu[...] = jnp.zeros((N, N), F32)
 
     pl.semaphore_wait(barrier, count)
 
@@ -336,7 +344,8 @@
         take_rest(2 + 2 * k)
         return carry
 
-    lax.fori_loop(0, jnp.maximum(level - 1, 0), early, 0)
+    below = jnp.minimum(level, 5)
+    lax.fori_loop(0, jnp.maximum(below - 1, 0), early, 0)
 
     left_slot = jnp.where(even, 2 * level - 1, 0)
 
@@ -347,7 +356,7 @@
 
         @pl.when(even)
         def _():
-            take(2 * level)
+            take(2 * below)
 
     take_last(take_lead)
 
@@ -360,24 +369,43 @@
         def _():
             to(sx0.at[0], xu.at[part_rows(part)], s_send.at[2], rx_recv.at[1, part], s, j).wait_recv()
 
-    factor_start(d2, f1b)
-    take_last(take_rest)
-    take_link(0)
-
-    def fill():
-        project(own_h, 0, v2, ycat, 2 * N, 8, f1b, zb)
-        for x, at, to_ in ((xl, 0, pl1), (xu, N, pu1)):
-            project(x, 0, v2, ycat, at, H, f1b, zb)
-            lead_start(v2, to_, at)
-
-    factor_rest(d2, {6: fill}, f1b, f2b, zb)
-    lead_end(v2, ycat, f2b, pl1, 0)
-    lead_end(v2, ycat, f2b, pu1, N)
+    def first_lead():
+        return to(pl1, rc1.at[12], s_send.at[4], r1_recv.at[12], 32, j)
+
+    def first_rest():
+        return to(pl2, rc2.at[12], s_send.at[6], r2_recv.at[12], 32, j)
+
+    @pl.when(s == 0)
+    def _():
+        pl1[...] = d2[0:H, 0:H]
+        first_lead().start()
+        take_last(take_rest)
+        pl2[0:H, :] = d2[H:N, :]
+        pl2[H : H + 8, :] = own_h[...]
+        first_rest().start()
+
+    @pl.when(inner)
+    def _():
+        factor_start(d2, f1b)
+        take_last(take_rest)
+        take_link(0)
+
+        def fill():
+            project(own_h, 0, v2, ycat, 2 * N, 8, f1b, zb)
+            for x, at, to_ in ((xl, 0, pl1), (xu, N, pu1)):
+                project(x, 0, v2, ycat, at, H, f1b, zb)
+                lead_start(v2, to_, at)
+
+        factor_rest(d2, {6: fill}, f1b, f2b, zb)
+        lead_end(v2, ycat, f2b, pl1, 0)
+        lead_end(v2, ycat, f2b, pu1, N)
+
+    sending = inner & jnp.logical_not(root)
 
     lower_slot, upper_slot = 2 + 2 * level, 1 + 2 * level
 
     def lead_sends(act):
-        @pl.when(inner)
+        @pl.when(sending)
         def _():
             act(to(pl1, rc1.at[lower_slot], s_send.at[4], r1_recv.at[lower_slot], s - dist, j))
 
@@ -386,7 +414,7 @@
             act(to(pu1, rc1.at[upper_slot], s_send.at[5], r1_recv.at[upper_slot], s + dist, j))
 
     def rest_sends(act):
-        @pl.when(inner)
+        @pl.when(sending)
         def _():
             act(to(pl2, rc2.at[lower_slot], s_send.at[6], r2_recv.at[lower_slot], s - dist, j))
 
@@ -407,12 +435,16 @@
 
     lead_sends(lambda c: c.start())
     take_link(1)
-    for x, at in ((xl, H), (xu, N + H)):
-        project(x, H, v2, ycat, at, H, f1b, zb)
-        finish_rows(v2, ycat, f2b, at, H)
-    finish_rows(v2, ycat, f2b, 2 * N, 8)
-    rest_products(v2, pl2, 0)
-    rest_products(v2, pu2, N)
+
+    @pl.when(inner)
+    def _():
+        for x, at in ((xl, H), (xu, N + H)):
+            project(x, H, v2, ycat, at, H, f1b, zb)
+            finish_rows(v2, ycat, f2b, at, H)
+        finish_rows(v2, ycat, f2b, 2 * N, 8)
+        rest_products(v2, pl2, 0)
+        rest_products(v2, pu2, N)
+
     rest_sends(lambda c: c.start())
 
     for part in range(2):
@@ -427,8 +459,7 @@
 
         link_send(part, lambda c: c.start())
 
-    @pl.when(inner)
-    def _():
+    def own_means():
         lo, hi = means(v2, f1b, f2b, zb)
         gb[:, 0:H] = lo
         gb[:, H:N] = hi
@@ -438,12 +469,38 @@
         ga[:, 0:H] = lo
         ga[:, H:N] = hi
 
-    @pl.when(s > 0)
-    def _():
+    def spread_first(act):
+        for a, seg in enumerate((16, 8, 4, 2, 1, 0)):
+            act(to(xfirst, xin.at[0], x_send.at[13 + a], x_recv.at[0], seg, j))
+
+    @pl.when(root)
+    def _():
+        to(pl1, rc1.at[12], s_send.at[4], r1_recv.at[12], s, j).wait_recv()
+        to(pl2, rc2.at[12], s_send.at[6], r2_recv.at[12], s, j).wait_recv()
+        d1[0:H, 0:H] = rc1[12] - pl1[...]
+        d1[H:N, :] = rc2[12, 0:H, :] - pl2[0:H, :]
+        h1[...] = rc2[12, H : H + 8, :] - pl2[H : H + 8, :]
+        factor_start(d1, f1c)
+
+        def fill():
+            project(h1, 0, hv, hy, 0, 8, f1c, zc)
+            own_means()
+
+        factor_rest(d1, {2: fill}, f1c, f2c, zc)
+        finish_rows(hv, hy, f2c, 0, 8)
+        lo, hi = means(hv, f1c, f2c, zc)
+        xfirst[:, 0:H] = lo
+        xfirst[:, H:N] = hi
+        spread_first(lambda c: c.start())
+        xown[...] = gb[2 * N : 2 * N + 8, :] - nn(xfirst[...], gb[0:N, :])
+
+    @pl.when(jnp.logical_not(root))
+    def _():
+        @pl.when(inner)
+        def _():
+            own_means()
+
         early_means()
-
-    @pl.when(inner)
-    def _():
         to(xown, xin.at[0], x_send.at[0], x_recv.at[0], s, j).wait_recv()
 
     @pl.when(upper)
@@ -456,11 +513,9 @@
 
     @pl.when(s == 0)
     def _():
-        lo, hi = means(v2[2 * N : 2 * N + 8, :], f1b, f2b, zb)
-        xown[:, 0:H] = lo
-        xown[:, H:N] = hi
-
-    @pl.when(s > 0)
+        xown[...] = xin[0]
+
+    @pl.when(sending)
     def _():
         xown[...] = gb[2 * N : 2 * N + 8, :] - (
             nn(xin[0], gb[0:N, :]) + nn(xin[1], gb[N : 2 * N, :])
@@ -470,14 +525,10 @@
         def step(i, d):
             k = level - 1 - i
             act(to(xown, xin.at[0], x_send.at[2 * k], x_recv.at[0], s + d, j))
-
-            @pl.when(inner)
-            def _():
-                act(to(xown, xin.at[1], x_send.at[2 * k + 1], x_recv.at[1], s - d, j))
-
+            act(to(xown, xin.at[1], x_send.at[2 * k + 1], x_recv.at[1], s - d, j))
             return d // 2
 
-        lax.fori_loop(0, level, step, dist // 2)
+        lax.fori_loop(0, jnp.where(inner, level, 0), step, dist // 2)
 
         @pl.when(jnp.logical_not(even))
         def _():
@@ -485,7 +536,7 @@
 
     spread(lambda c: c.start())
 
-    @pl.when(s == 0)
+    @pl.when(root)
     def _():
         early_means()
 
@@ -517,6 +568,15 @@
     up0_link(lambda c: c.wait_send())
     up0_rest(lambda c: c.wait_send())
 
+
+    @pl.when(s == 0)
+    def _():
+        first_lead().wait_send()
+        first_rest().wait_send()
+
+    @pl.when(root)
+    def _():
+        spread_first(lambda c: c.wait_send())
 
     lead_sends(lambda c: c.wait_send())
     for part in range(2):
@@ -542,12 +602,13 @@
         out_specs=pl.BlockSpec(memory_space=vmem),
         scratch_shapes=[
             square, square, square, vmem((64, N), F32), square, square, square, square, vmem((8, N), F32), vmem((2 * N + 8, H), F32), tall, tall,
-            half, half, half, half, half, half, tall, tall,
+            half, half, half, half, half, half, half, half, half,
+            vmem((8, N), F32), vmem((8, H), F32), vmem((8, N), F32), tall, tall,
             vmem((8, N), F32), vmem((13, H, H), F32), vmem((13, H + 8, N), F32),
             half, slab, pair, half, slab, half, slab, pair,
             vmem((3, 8, N), F32), vmem((8, N), F32),
             dma((6, 8)), dma((6, 8)),
-            dma((13,)), dma((13,)), dma((2, 2)), dma((10,)), dma((13,)), dma((3,)), dma((6,)),
+            dma((13,)), dma((13,)), dma((2, 2)), dma((10,)), dma((19,)), dma((3,)), dma((6,)),
         ],
         compiler_params=pltpu.CompilerParams(
             collective_id=0, has_side_effects=True, vmem_limit_bytes=32 * 1024 * 1024

time: 158 us -> 149 us (0.943)
  Pallas kernels: 154 us -> 145 us
    pallas_call x1, Pallas kernels: 154 us -> 145 us  [body(): pl.pallas_call(kernel, out_shape=jax.ShapeDtypeStruct((2, 32), F32), in_s...]
where the time goes in v7:
time: 149 us
  Pallas kernels  145 us (97%)
  local copies, waits for them, and re-layouts  3.15 us (2%)
    pallas_call x1, Pallas kernels, body(): pl.pallas_call(kernel, out_shape=jax.ShapeDtypeStruct((2, 32), F32), in_s...  145 us

profile of v7, /device:TPU:16, one launch (start us, length us, event | category | flops | bytes accessed | tf_op | source)
XLA Modules:
  0.0 148.6 jit_solution(7404799016010041924)
XLA Ops:
  0.0 0.0 copy-start.2
  0.0 0.7 copy-done.2
  0.7 0.2 dynamic_update_slice.3.info
  0.9 0.0 copy-start
  0.9 0.8 copy-done
  1.8 0.0 copy-start.1
  1.8 0.8 copy-done.1
  2.6 145.4 %shard_map.37 = f32[2,32]{1,0:T(2,128)S(1)} custom-call(f32[2,32,256]{2,1,0:T(8,128)S(1)} %copy-done, f32[2,32,256]{2,1,0:T(8,128)S(1)} %copy-done.1, f32[8,256]{1,0:T(8,128)S(1)} %dynamic_update_slice.3.info), custom_call_target="tpu_custom_call" | custom-call | tf_op jit(solution)/shard_map/pallas_call | solution.py:598
  148.0 0.6 copy.6
  (1 shorter events, 0.0 us)
Async XLA Ops:
  0.0 0.7 copy-start.2
  0.9 0.8 copy-start
  1.8 0.8 copy-start.1

commit v8 on v7

--- a/solution.py
+++ b/solution.py
@@ -115,6 +115,20 @@
     to[H : H + 8, :] = nt(v[2 * N : 2 * N + 8, :], v[at : at + N, :])
 
 
+def rest_rows(v, at, cols):
+    return jnp.concatenate([v[at + H : at + N, cols], v[2 * N : 2 * N + 8, cols]], axis=0)
+
+
+def rest_start(v, to, at):
+    c = slice(0, H)
+    to[...] = nt(rest_rows(v, at, c), v[at : at + N, c])
+
+
+def rest_end(v, to, at):
+    c = slice(H, N)
+    to[...] = to[...] + nt(rest_rows(v, at, c), v[at : at + N, c])
+
+
 def finish_rows(v, y, f2, at, n):
     v[at : at + n, H:N] = nt(y[at : at + n, :], f2[...])
 
@@ -127,7 +141,7 @@
 
 def kernel(
     diag, coup, info, out,
-    d1, c0, c1, hin, d2, xl, xu, c1t, h1, ycat, v1, v2, f1a, f2a, za, f1b, f2b, zb, f1c, f2c, zc, hv, hy, xfirst, ga, gb,
+    d1, c0, c1, hin, d2, xl, xu, c1t, h1, ycat, v1, v2, f1a, f2a, za, f1b, f2b, zb, f1c, f2c, zc, hv, hy, xfirst, placed, ga, gb,
     own_h, rc1, rc2, pu01, pu02, sx0, pl1, pl2, pu1, pu2, sx, xin, xown,
     g1_send, g1_recv, r1_recv, r2_recv, rx_recv, s_send, x_send, x_recv, own_sem,
 ):
@@ -190,10 +204,17 @@
         (diag.at[1, :, 0:H], d1.at[rows, 0:H]),
         (coup.at[0], c0.at[rows]),
         (coup.at[1], c1.at[rows]),
-        (info, hin.at[pl.ds(pl.multiple_of(j * 8, 8), 8)]),
+        (placed, hin.at[pl.ds(pl.multiple_of(j * 8, 8), 8)]),
         (diag.at[0], d2.at[rows]),
         (diag.at[1, :, H:N], d1.at[rows, H:N]),
     ]
+    placed[...] = jnp.zeros((8, N), F32)
+    for i in range(8):
+
+        @pl.when(j == i)
+        def _():
+            placed[0:2, 32 * i : 32 * i + 32] = info[...]
+
     local = [
         pltpu.make_async_copy(src, dst, own_sem.at[a]) for a, (src, dst) in enumerate(first)
     ]
@@ -389,14 +410,19 @@
         factor_start(d2, f1b)
         take_last(take_rest)
         take_link(0)
+        take_link(1)
 
         def fill():
             project(own_h, 0, v2, ycat, 2 * N, 8, f1b, zb)
             for x, at, to_ in ((xl, 0, pl1), (xu, N, pu1)):
-                project(x, 0, v2, ycat, at, H, f1b, zb)
+                project(x, 0, v2, ycat, at, N, f1b, zb)
                 lead_start(v2, to_, at)
 
-        factor_rest(d2, {6: fill}, f1b, f2b, zb)
+        def fill_rest():
+            rest_start(v2, pl2, 0)
+            rest_start(v2, pu2, N)
+
+        factor_rest(d2, {2: fill, 9: fill_rest}, f1b, f2b, zb)
         lead_end(v2, ycat, f2b, pl1, 0)
         lead_end(v2, ycat, f2b, pu1, N)
 
@@ -434,16 +460,13 @@
             act(to(sx.at[part], xl.at[at], s_send.at[8 + part], rx_recv.at[0, part], s + dist, j))
 
     lead_sends(lambda c: c.start())
-    take_link(1)
-
     @pl.when(inner)
     def _():
-        for x, at in ((xl, H), (xu, N + H)):
-            project(x, H, v2, ycat, at, H, f1b, zb)
+        for at in (H, N + H):
             finish_rows(v2, ycat, f2b, at, H)
         finish_rows(v2, ycat, f2b, 2 * N, 8)
-        rest_products(v2, pl2, 0)
-        rest_products(v2, pu2, N)
+        rest_end(v2, pl2, 0)
+        rest_end(v2, pu2, N)
 
     rest_sends(lambda c: c.start())
 
@@ -501,25 +524,36 @@
             own_means()
 
         early_means()
-        to(xown, xin.at[0], x_send.at[0], x_recv.at[0], s, j).wait_recv()
-
-    @pl.when(upper)
-    def _():
-        to(xown, xin.at[1], x_send.at[0], x_recv.at[1], s, j).wait_recv()
-
-    @pl.when(jnp.logical_not(upper))
-    def _():
+
+    def wait_mean(a):
+        to(xown, xin.at[a], x_send.at[0], x_recv.at[a], s, j).wait_recv()
+
+    @pl.when(s == 0)
+    def _():
+        wait_mean(0)
+        xown[...] = xin[0]
         xin[1] = jnp.zeros((8, N), F32)
 
-    @pl.when(s == 0)
-    def _():
-        xown[...] = xin[0]
-
-    @pl.when(sending)
-    def _():
-        xown[...] = gb[2 * N : 2 * N + 8, :] - (
-            nn(xin[0], gb[0:N, :]) + nn(xin[1], gb[N : 2 * N, :])
-        )
+    @pl.when(to_lower)
+    def _():
+        @pl.when(upper)
+        def _():
+            wait_mean(1)
+
+        @pl.when(jnp.logical_not(upper))
+        def _():
+            xin[1] = jnp.zeros((8, N), F32)
+
+        xown[...] = gb[2 * N : 2 * N + 8, :] - nn(xin[1], gb[N : 2 * N, :])
+        wait_mean(0)
+        xown[...] = xown[...] - nn(xin[0], gb[0:N, :])
+
+    @pl.when(to_upper)
+    def _():
+        wait_mean(0)
+        xown[...] = gb[2 * N : 2 * N + 8, :] - nn(xin[0], gb[0:N, :])
+        wait_mean(1)
+        xown[...] = xown[...] - nn(xin[1], gb[N : 2 * N, :])
 
     def spread(act):
         def step(i, d):
@@ -586,8 +620,6 @@
 
 
 def body(diagonal, coupling, info):
-    offset = lax.axis_index("state") * 32
-    placed = lax.dynamic_update_slice(jnp.zeros((8, N), F32), info, (0, offset))
     vmem = pltpu.VMEM
     dma = pltpu.SemaphoreType.DMA
     square = vmem((N, N), F32)
@@ -598,12 +630,12 @@
     return pl.pallas_call(
         kernel,
         out_shape=jax.ShapeDtypeStruct((2, 32), F32),
-        in_specs=[pl.BlockSpec(memory_space=pltpu.HBM)] * 3,
+        in_specs=[pl.BlockSpec(memory_space=m) for m in (pltpu.HBM, pltpu.HBM, vmem)],
         out_specs=pl.BlockSpec(memory_space=vmem),
         scratch_shapes=[
             square, square, square, vmem((64, N), F32), square, square, square, square, vmem((8, N), F32), vmem((2 * N + 8, H), F32), tall, tall,
             half, half, half, half, half, half, half, half, half,
-            vmem((8, N), F32), vmem((8, H), F32), vmem((8, N), F32), tall, tall,
+            vmem((8, N), F32), vmem((8, H), F32), vmem((8, N), F32), vmem((8, N), F32), tall, tall,
             vmem((8, N), F32), vmem((13, H, H), F32), vmem((13, H + 8, N), F32),
             half, slab, pair, half, slab, half, slab, pair,
             vmem((3, 8, N), F32), vmem((8, N), F32),
@@ -613,7 +645,7 @@
         compiler_params=pltpu.CompilerParams(
             collective_id=0, has_side_effects=True, vmem_limit_bytes=32 * 1024 * 1024
         ),
-    )(diagonal, coupling, placed)
+    )(diagonal, coupling, info)
 
 
 def solution(mesh):

time: 149 us -> 159 us (1.067)
  Pallas kernels: 145 us -> 156 us
    pallas_call x1, Pallas kernels: 145 us -> 156 us  [body(): pl.pallas_call(kernel, out_shape=jax.ShapeDtypeStruct((2, 32), F32), in_s...]
where the time goes in v8:
time: 159 us
  Pallas kernels  156 us (98%)
  local copies, waits for them, and re-layouts  2.92 us (2%)
    pallas_call x1, Pallas kernels, body(): pl.pallas_call(kernel, out_shape=jax.ShapeDtypeStruct((2, 32), F32), in_s...  156 us

profile of v8, /device:TPU:16, one launch (start us, length us, event | category | flops | bytes accessed | tf_op | source)
XLA Modules:
  0.0 158.7 jit_solution(16990761176730999398)
XLA Ops:
  0.0 0.0 copy-start
  0.0 0.8 copy-done
  0.8 0.0 copy-start.1
  0.8 0.8 copy-done.1
  1.7 0.0 copy-start.2
  1.7 0.7 copy-done.2
  2.4 155.8 %shard_map.37 = f32[2,32]{1,0:T(2,128)S(1)} custom-call(f32[2,32,256]{2,1,0:T(8,128)S(1)} %copy-done, f32[2,32,256]{2,1,0:T(8,128)S(1)} %copy-done.1, f32[2,32]{1,0:T(2,128)S(1)} %copy-done.2), custom_call_target="tpu_custom_call" | custom-call | tf_op jit(solution)/shard_map/pallas_call | solution.py:630
  158.2 0.6 copy.5
Async XLA Ops:
  0.0 0.8 copy-start
  0.8 0.8 copy-start.1
  1.7 0.7 copy-start.2

commit v9 on v8

--- a/solution.py
+++ b/solution.py
@@ -410,19 +410,21 @@
         factor_start(d2, f1b)
         take_last(take_rest)
         take_link(0)
-        take_link(1)
 
         def fill():
             project(own_h, 0, v2, ycat, 2 * N, 8, f1b, zb)
             for x, at, to_ in ((xl, 0, pl1), (xu, N, pu1)):
-                project(x, 0, v2, ycat, at, N, f1b, zb)
+                project(x, 0, v2, ycat, at, H, f1b, zb)
                 lead_start(v2, to_, at)
 
         def fill_rest():
+            take_link(1)
+            for x, at in ((xl, H), (xu, N + H)):
+                project(x, H, v2, ycat, at, H, f1b, zb)
             rest_start(v2, pl2, 0)
             rest_start(v2, pu2, N)
 
-        factor_rest(d2, {2: fill, 9: fill_rest}, f1b, f2b, zb)
+        factor_rest(d2, {2: fill, 8: fill_rest}, f1b, f2b, zb)
         lead_end(v2, ycat, f2b, pl1, 0)
         lead_end(v2, ycat, f2b, pu1, N)
 

time: 159 us -> 143 us (0.90)
  Pallas kernels: 156 us -> 140 us
    pallas_call x1, Pallas kernels: 156 us -> 140 us  [body(): pl.pallas_call(kernel, out_shape=jax.ShapeDtypeStruct((2, 32), F32), in_s...]
where the time goes in v9:
time: 143 us
  Pallas kernels  140 us (98%)
  local copies, waits for them, and re-layouts  2.92 us (2%)
    pallas_call x1, Pallas kernels, body(): pl.pallas_call(kernel, out_shape=jax.ShapeDtypeStruct((2, 32), F32), in_s...  140 us
    unnamed x7, local copies, waits for them, and re-layouts  2.92 us

profile of v9, /device:TPU:16, one launch (start us, length us, event | category | flops | bytes accessed | tf_op | source)
XLA Modules:
  0.0 142.5 jit_solution(6627147419319871098)
XLA Ops:
  0.0 0.0 copy-start
  0.0 0.8 copy-done
  0.8 0.0 copy-start.1
  0.8 0.8 copy-done.1
  1.7 0.0 copy-start.2
  1.7 0.7 copy-done.2
  2.4 139.6 %shard_map.37 = f32[2,32]{1,0:T(2,128)S(1)} custom-call(f32[2,32,256]{2,1,0:T(8,128)S(1)} %copy-done, f32[2,32,256]{2,1,0:T(8,128)S(1)} %copy-done.1, f32[2,32]{1,0:T(2,128)S(1)} %copy-done.2), custom_call_target="tpu_custom_call" | custom-call | tf_op jit(solution)/shard_map/pallas_call | solution.py:632
  142.0 0.6 copy.5
Async XLA Ops:
  0.0 0.8 copy-start
  0.8 0.8 copy-start.1
  1.7 0.7 copy-start.2

commit v10 on v9

--- a/solution.py
+++ b/solution.py
@@ -141,9 +141,9 @@
 
 def kernel(
     diag, coup, info, out,
-    d1, c0, c1, hin, d2, xl, xu, c1t, h1, ycat, v1, v2, f1a, f2a, za, f1b, f2b, zb, f1c, f2c, zc, hv, hy, xfirst, placed, ga, gb,
+    d1, c0, c1, hin, d2, xl, xu, c1t, h1, ycat, v1, v2, f1a, f2a, za, f1b, f2b, zb, f1c, f2c, zc, hv, hy, xfirst, placed, gat, cols, cols_in, fold, fold_in, ga, gb,
     own_h, rc1, rc2, pu01, pu02, sx0, pl1, pl2, pu1, pu2, sx, xin, xown,
-    g1_send, g1_recv, r1_recv, r2_recv, rx_recv, s_send, x_send, x_recv, own_sem,
+    g1_send, g1_recv, r1_recv, r2_recv, rx_recv, s_send, x_send, x_recv, own_sem, fold_send, fold_recv,
 ):
     s = lax.axis_index("tm")
     j = lax.axis_index("state")
@@ -462,7 +462,7 @@
             act(to(sx.at[part], xl.at[at], s_send.at[8 + part], rx_recv.at[0, part], s + dist, j))
 
     lead_sends(lambda c: c.start())
-    @pl.when(inner)
+    @pl.when(sending)
     def _():
         for at in (H, N + H):
             finish_rows(v2, ycat, f2b, at, H)
@@ -494,6 +494,17 @@
         ga[:, 0:H] = lo
         ga[:, H:N] = hi
 
+    def columns_up():
+        return to(cols, cols_in, fold_send.at[0], fold_recv.at[0], s + 1, j)
+
+    def folded_down():
+        return to(fold, fold_in, fold_send.at[1], fold_recv.at[1], s - 1, j)
+
+    def columns():
+        gat[...] = ga[N : 2 * N, :].T
+        cols[...] = gat[rows, :]
+        columns_up().start()
+
     def spread_first(act):
         for a, seg in enumerate((16, 8, 4, 2, 1, 0)):
             act(to(xfirst, xin.at[0], x_send.at[13 + a], x_recv.at[0], seg, j))
@@ -503,6 +514,10 @@
         to(pl1, rc1.at[12], s_send.at[4], r1_recv.at[12], s, j).wait_recv()
         to(pl2, rc2.at[12], s_send.at[6], r2_recv.at[12], s, j).wait_recv()
         d1[0:H, 0:H] = rc1[12] - pl1[...]
+        finish_rows(v2, ycat, f2b, H, H)
+        finish_rows(v2, ycat, f2b, N, N)
+        finish_rows(v2, ycat, f2b, 2 * N, 8)
+        rest_end(v2, pl2, 0)
         d1[H:N, :] = rc2[12, 0:H, :] - pl2[0:H, :]
         h1[...] = rc2[12, H : H + 8, :] - pl2[H : H + 8, :]
         factor_start(d1, f1c)
@@ -527,6 +542,18 @@
 
         early_means()
 
+    @pl.when(even & jnp.logical_not(root))
+    def _():
+        columns()
+
+    @pl.when(jnp.logical_not(even))
+    def _():
+        to(cols, cols_in, fold_send.at[0], fold_recv.at[0], s, j).wait_recv()
+        fold[0:32, :] = nt(cols_in[...], gb[0:N, :])
+        fold[32:64, :] = nt(cols_in[...], gb[N : 2 * N, :])
+        fold[64:72, :] = gb[2 * N : 2 * N + 8, :]
+        folded_down().start()
+
     def wait_mean(a):
         to(xown, xin.at[a], x_send.at[0], x_recv.at[a], s, j).wait_recv()
 
@@ -566,33 +593,47 @@
 
         lax.fori_loop(0, jnp.where(inner, level, 0), step, dist // 2)
 
-        @pl.when(jnp.logical_not(even))
-        def _():
-            act(to(xown, xin.at[2], x_send.at[12], x_recv.at[2], s - 1, j))
+        @pl.when(even & inner)
+        def _():
+            act(to(xown, xin.at[2], x_send.at[12], x_recv.at[2], s - 2, j))
 
     spread(lambda c: c.start())
 
     @pl.when(root)
     def _():
         early_means()
+        columns()
 
     part = ga[2 * N : 2 * N + 8, :] - nn(xown[...], ga[0:N, :])
 
+    def put(later):
+        both = jnp.concatenate([xown[0:1, :], later[0:1, :]], axis=0)
+        for i in range(8):
+
+            @pl.when(j == i)
+            def _():
+                out[...] = both[:, 32 * i : 32 * i + 32]
+
+    @pl.when(jnp.logical_not(even))
+    def _():
+        put(part - nn(xin[1], ga[N : 2 * N, :]))
+
     @pl.when(even)
     def _():
-        to(xown, xin.at[2], x_send.at[12], x_recv.at[2], s, j).wait_recv()
-
-    @pl.when(jnp.logical_not(even))
-    def _():
-        xin[2] = xin[1]
-
-    later = part - nn(xin[2], ga[N : 2 * N, :])
-    both = jnp.concatenate([xown[0:1, :], later[0:1, :]], axis=0)
-    for i in range(8):
-
-        @pl.when(j == i)
-        def _():
-            out[...] = both[:, 32 * i : 32 * i + 32]
+        put(part)
+        to(fold, fold_in, fold_send.at[1], fold_recv.at[1], s, j).wait_recv()
+        share = nt(xown[...], fold_in[0:32, :]) - nt(fold_in[64:72, :], cols[...])
+
+        @pl.when(s < 62)
+        def _():
+            to(xown, xin.at[2], x_send.at[12], x_recv.at[2], s, j).wait_recv()
+
+        @pl.when(s == 62)
+        def _():
+            xin[2] = jnp.zeros((8, N), F32)
+
+        share = share + nt(xin[2], fold_in[32:64, :])
+        out[1:2, :] = out[1:2, :] + share[0:1, :]
 
     gather(3, lambda c: c.wait_send())
     for a in (1, 2, 4):
@@ -613,6 +654,14 @@
     @pl.when(root)
     def _():
         spread_first(lambda c: c.wait_send())
+
+    @pl.when(even)
+    def _():
+        columns_up().wait_send()
+
+    @pl.when(jnp.logical_not(even))
+    def _():
+        folded_down().wait_send()
 
     lead_sends(lambda c: c.wait_send())
     for part in range(2):
@@ -637,12 +686,13 @@
         scratch_shapes=[
             square, square, square, vmem((64, N), F32), square, square, square, square, vmem((8, N), F32), vmem((2 * N + 8, H), F32), tall, tall,
             half, half, half, half, half, half, half, half, half,
-            vmem((8, N), F32), vmem((8, H), F32), vmem((8, N), F32), vmem((8, N), F32), tall, tall,
+            vmem((8, N), F32), vmem((8, H), F32), vmem((8, N), F32), vmem((8, N), F32),
+            square, vmem((32, N), F32), vmem((32, N), F32), vmem((72, N), F32), vmem((72, N), F32), tall, tall,
             vmem((8, N), F32), vmem((13, H, H), F32), vmem((13, H + 8, N), F32),
             half, slab, pair, half, slab, half, slab, pair,
             vmem((3, 8, N), F32), vmem((8, N), F32),
             dma((6, 8)), dma((6, 8)),
-            dma((13,)), dma((13,)), dma((2, 2)), dma((10,)), dma((19,)), dma((3,)), dma((6,)),
+            dma((13,)), dma((13,)), dma((2, 2)), dma((10,)), dma((19,)), dma((3,)), dma((6,)), dma((2,)), dma((2,)),
         ],
         compiler_params=pltpu.CompilerParams(
             collective_id=0, has_side_effects=True, vmem_limit_bytes=32 * 1024 * 1024

time: 143 us -> 140 us (0.979)
  the two profiles are of different devices: /device:TPU:16 before, /device:TPU:8 now
where the time goes in v10:
time: 140 us; the launch traced here: 139 us
  Pallas kernels  136 us (97%)
  local copies, waits for them, and re-layouts  2.92 us (2%)
    pallas_call x1, Pallas kernels, body(): pl.pallas_call(kernel, out_shape=jax.ShapeDtypeStruct((2, 32), F32), in_s...  136 us
    unnamed x7, local copies, waits for them, and re-layouts  2.92 us

profile of v10, /device:TPU:8, one launch (start us, length us, event | category | flops | bytes accessed | tf_op | source)
XLA Modules:
  0.0 139.3 jit_solution(2667185915893199640)
XLA Ops:
  0.0 0.0 copy-start
  0.0 0.8 copy-done
  0.8 0.0 copy-start.1
  0.8 0.8 copy-done.1
  1.7 0.0 copy-start.2
  1.7 0.7 copy-done.2
  2.4 136.4 %shard_map.37 = f32[2,32]{1,0:T(2,128)S(1)} custom-call(f32[2,32,256]{2,1,0:T(8,128)S(1)} %copy-done, f32[2,32,256]{2,1,0:T(8,128)S(1)} %copy-done.1, f32[2,32]{1,0:T(2,128)S(1)} %copy-done.2), custom_call_target="tpu_custom_call" | custom-call | tf_op jit(solution)/shard_map/pallas_call | solution.py:681
  138.8 0.6 copy.5
Async XLA Ops:
  0.0 0.8 copy-start
  0.8 0.8 copy-start.1
  1.7 0.7 copy-start.2

commit v11 on v10

--- a/solution.py
+++ b/solution.py
@@ -441,11 +441,12 @@
         def _():
             act(to(pu1, rc1.at[upper_slot], s_send.at[5], r1_recv.at[upper_slot], s + dist, j))
 
-    def rest_sends(act):
+    def rest_down(act):
         @pl.when(sending)
         def _():
             act(to(pl2, rc2.at[lower_slot], s_send.at[6], r2_recv.at[lower_slot], s - dist, j))
 
+    def rest_up(act):
         @pl.when(upper)
         def _():
             act(to(pu2, rc2.at[upper_slot], s_send.at[7], r2_recv.at[upper_slot], s + dist, j))
@@ -467,10 +468,25 @@
         for at in (H, N + H):
             finish_rows(v2, ycat, f2b, at, H)
         finish_rows(v2, ycat, f2b, 2 * N, 8)
+
+    def rest_lower():
         rest_end(v2, pl2, 0)
+        rest_down(lambda c: c.start())
+
+    def rest_upper():
         rest_end(v2, pu2, N)
-
-    rest_sends(lambda c: c.start())
+        rest_up(lambda c: c.start())
+
+    @pl.when(to_lower)
+    def _():
+        rest_lower()
+        rest_upper()
+
+    @pl.when(to_upper)
+    def _():
+        rest_upper()
+        rest_lower()
+
 
     for part in range(2):
 
@@ -666,7 +682,8 @@
     lead_sends(lambda c: c.wait_send())
     for part in range(2):
         link_send(part, lambda c: c.wait_send())
-    rest_sends(lambda c: c.wait_send())
+    rest_down(lambda c: c.wait_send())
+    rest_up(lambda c: c.wait_send())
     spread(lambda c: c.wait_send())
 
 

time: 140 us -> 139 us (level)
  no operation moved by 1% of the time
where the time goes in v11:
time: 139 us
  Pallas kernels  136 us (98%)
  local copies, waits for them, and re-layouts  2.92 us (2%)
    pallas_call x1, Pallas kernels, body(): pl.pallas_call(kernel, out_shape=jax.ShapeDtypeStruct((2, 32), F32), in_s...  136 us
    unnamed x7, local copies, waits for them, and re-layouts  2.92 us

profile of v11, /device:TPU:8, one launch (start us, length us, event | category | flops | bytes accessed | tf_op | source)
XLA Modules:
  0.0 138.7 jit_solution(433951877051613137)
XLA Ops:
  0.0 0.0 copy-start
  0.0 0.8 copy-done
  0.8 0.0 copy-start.1
  0.8 0.8 copy-done.1
  1.7 0.0 copy-start.2
  1.7 0.7 copy-done.2
  2.4 135.8 %shard_map.37 = f32[2,32]{1,0:T(2,128)S(1)} custom-call(f32[2,32,256]{2,1,0:T(8,128)S(1)} %copy-done, f32[2,32,256]{2,1,0:T(8,128)S(1)} %copy-done.1, f32[2,32]{1,0:T(2,128)S(1)} %copy-done.2), custom_call_target="tpu_custom_call" | custom-call | tf_op jit(solution)/shard_map/pallas_call | solution.py:698
  138.1 0.6 copy.5
Async XLA Ops:
  0.0 0.8 copy-start
  0.8 0.8 copy-start.1
  1.7 0.7 copy-start.2
